TPU v7x, 32 devices: a whole 2x2x4 slice. The times are simulated.
32 devices in a mesh: lat: 2 (over y), comp: 16 (over z, x, core).
Axes of the slice: x: 2, y: 2, z: 4, core: 2. Of those that a mesh axis runs over, the one named last changes fastest.
Arguments:
- spectrum: float32 [1152, 32, 1024], P('comp', 'lat'), may hold values from -4 to 4
- interp_plus: float32 [1152, 1152], P('lat'), may hold values from -0.1875 to 0.1875
- interp_minus: float32 [1152, 1152], P('lat'), may hold values from -0.1875 to 0.1875
- source_gain: float32 [1152], replicated, may hold values from 0.05 to 0.3
- current: float32 [2, 32, 1024], P(None, 'lat'), may hold values from -0.2 to 0.2
- sea_mask: int32 [32, 1024], P('lat'), may hold values 0 or 1
- limiter_flags: int32 [32, 1024], P('lat'), may hold values 0 or 1
- ice_cells: int32 [1024], replicated, may hold values from 0 to 32767
Outputs:
- spectrum_out: float32 [1152, 32, 1024], P('comp', 'lat')
Inputs may be any that keep to these rules, and one draw needn't show every extreme that they name: `ice_cells`: indices may repeat.
All inputs are finite; a program needn't handle non-finite values. No bound on the sum of `sea_mask` or of `limiter_flags` on one device may be relied on, other than what follows from the above.
Results may differ from a plain program's by a relative error of at most 0.0003.
Values sent between devices are 32-bit elements; how exact they have to be, the bound alone decides.
A program may use at most 128 MiB of HBM per device.

v0:
```python
import jax
import jax.numpy as jnp
from jax import lax
from jax.sharding import PartitionSpec as P

ND = 36
NF = 32
K = 1152
OUTER = 2
SUB = 2


def padded_2(cells, sides, width):
    for axis, dim in sides:
        count = lax.axis_size(axis)
        ends = count - 1
        head = lax.slice_in_dim(cells, 0, width, axis=dim)
        tail = lax.slice_in_dim(cells, cells.shape[dim] - width, cells.shape[dim], axis=dim)
        cells = jnp.concatenate(
            [
                lax.ppermute(tail, axis, [(i, (i + 1) % count) for i in range(ends)]),
                cells,
                lax.ppermute(head, axis, [((i + 1) % count, i) for i in range(ends)]),
            ],
            axis=dim,
        )
    return cells


def minmod(first, second):
    return 0.5 * (jnp.sign(first) + jnp.sign(second)) * jnp.minimum(jnp.abs(first), jnp.abs(second))


def speeds(index):
    direction = (index // NF).astype(jnp.float32)
    frequency = (index % NF).astype(jnp.float32)
    angle_dir = 2.0 * jnp.pi * (direction + 0.5) / ND
    magnitude = 0.35 * (0.5 + 0.5 * frequency / (NF - 1))
    return (
        (magnitude * jnp.cos(angle_dir))[:, None, None],
        (magnitude * jnp.sin(angle_dir))[:, None, None],
    )


def advect(padded, statics, speed_x, speed_y):
    centre = padded[:, 1:-1]
    drift_x = statics[0]
    drift_y = statics[1]
    flagged = statics[2]
    wet = statics[3]
    east = jnp.roll(centre, -1, axis=2)
    west = jnp.roll(centre, 1, axis=2)
    slope_x = flagged * minmod(east - centre, centre - west)
    face_x = speed_x + 0.5 * (drift_x + jnp.roll(drift_x, -1, axis=1))
    flux_x = jnp.where(
        face_x >= 0.0,
        face_x * (centre + 0.5 * (1.0 - face_x) * slope_x),
        face_x * (east - 0.5 * (1.0 + face_x) * jnp.roll(slope_x, -1, axis=2)),
    )
    change_x = flux_x - jnp.roll(flux_x, 1, axis=2)
    slope_y = flagged * minmod(padded[:, 2:] - centre, centre - padded[:, :-2])
    face_y = speed_y + 0.5 * (drift_y[:-1] + drift_y[1:])
    flux_y = jnp.where(
        face_y >= 0.0,
        face_y * (centre[:, :-1] + 0.5 * (1.0 - face_y) * slope_y[:, :-1]),
        face_y * (centre[:, 1:] - 0.5 * (1.0 + face_y) * slope_y[:, 1:]),
    )
    change_y = flux_y[:, 1:] - flux_y[:, :-1]
    return wet[1:-1] * (centre[:, 1:-1] - change_x[:, 1:-1] - change_y)


def quartet(field, plus, minus, gain_col, keep):
    forcing = field * field * (plus + minus) - 2.0 * field * plus * minus
    update = gain_col * forcing / (1.0 + gain_col * (plus * plus + minus * minus))
    return (field + update) * keep


def ice_keep(ice_cells, offset, count):
    shifted = ice_cells - offset
    inside = (shifted >= 0) & (shifted < count)
    target = jnp.where(inside, shifted, count)
    iced = jnp.zeros((count + 1,), jnp.float32).at[target].set(1.0)[:count]
    return 1.0 - 0.6 * iced


def body(
    spectrum, interp_plus, interp_minus, source_gain, current, sea_mask, limiter_flags, ice_cells
):
    comp_count = lax.axis_size("comp")
    comp_rank = lax.axis_index("comp")
    lat_rank = lax.axis_index("lat")
    local_k, band_rows, lon_count = spectrum.shape
    band_cells = band_rows * lon_count
    points = band_cells // comp_count
    index = comp_rank * local_k + jnp.arange(local_k, dtype=jnp.int32)
    speed_x, speed_y = speeds(index)
    statics = jnp.stack(
        [current[0], current[1], limiter_flags.astype(jnp.float32), sea_mask.astype(jnp.float32)]
    )
    reach = 2 * SUB - 1
    rims = padded_2(statics, (("lat", 1),), reach)
    total_rows = rims.shape[1]
    narrow = rims[:, reach - 1 : total_rows - (reach - 1)]
    keep_own = ice_keep(ice_cells, lat_rank * band_cells + comp_rank * points, points)[None, :]
    gain_col = source_gain[:, None]
    plus_full, minus_full = (
        lax.all_gather(interp_plus, "lat", axis=0, tiled=True),
        lax.all_gather(interp_minus, "lat", axis=0, tiled=True),
    )
    field = spectrum
    for outer_step in range(OUTER):
        for sub_step in range(SUB):
            padded = padded_2(field, (("lat", 1),), 2)
            field = advect(padded, narrow, speed_x, speed_y)
        spread = field.reshape(local_k, comp_count, points)
        gathered = lax.all_to_all(spread, "comp", split_axis=1, concat_axis=0, tiled=True).reshape(
            K, points
        )
        plus = jnp.dot(
            plus_full, gathered, precision=lax.Precision.HIGHEST, preferred_element_type=jnp.float32
        )
        minus = jnp.dot(
            minus_full,
            gathered,
            precision=lax.Precision.HIGHEST,
            preferred_element_type=jnp.float32,
        )
        updated = quartet(gathered, plus, minus, gain_col, keep_own)
        returned = lax.all_to_all(
            updated.reshape(K, 1, points), "comp", split_axis=0, concat_axis=1, tiled=True
        )
        field = returned.reshape(local_k, band_rows, lon_count)
    return field


def solution(mesh):
    placed = (
        P("comp", "lat", None),
        P("lat", None),
        P("lat", None),
        P(),
        P(None, "lat", None),
        P("lat", None),
        P("lat", None),
        P(),
    )
    return jax.shard_map(
        body, mesh=mesh, in_specs=placed, out_specs=P("comp", "lat", None), check_vma=False
    )
```

profile of v0, /device:TPU:0, one launch (start us, length us, event | category | flops | bytes accessed | tf_op | source)
XLA Modules:
  0.0 948.4 jit_solution(1575838912205235534)
XLA Ops:
  6.5 3.0 fusion.118
  9.8 4.9 collective-permute-start.2
  14.9 1.3 collective-permute-start.3
  18.8 1.3 collective-permute-start.1
  20.1 4.6 collective-permute-start
  24.8 8.2 collective-permute-done.1
  34.2 7.6 constant_dynamic-update-slice_fusion.1
  42.0 5.7 fusion.113
  47.9 14.4 %multiply_multiply_fusion.7 = (f32[72,18,1024]{2,0,1:T(8,128)S(1)}, f32[72,18,1024]{2,0,1:T(8,128)}) fusion(f32[72,18,1023]{2,0,1:T(8,128)} %get-tuple-element.20, f32[72,18,1]{2,0,1:T(8,128)S(1)} %get-tuple-element.22, f32[72,20,1024]{2,0,1:T(8,128)S(1)} %get-tuple-element.34, f32[72,18,1]{2,0,1:T(8,128)S(1)} %get-tuple-element.21, ...), kind=kLoop, calls=%fused_computation.100 | loop fusion | flops 31850496 | bytes 37232640 | tf_op jit(solution)/shard_map/mul | solution.py:53
  62.4 3.8 slice.442
  66.2 5.0 fusion.3
  71.5 8.6 fusion.7
  80.1 7.0 fusion.75
  87.1 2.2 copy-done
  89.4 1.5 collective-permute-start.4
  90.9 1.3 collective-permute-start.5
  92.2 10.1 %collective-permute-done.4 = f32[72,2,1024]{2,0,1:T(8,128)S(1)} collective-permute-done((f32[72,2,1024]{2,0,1:T(8,128)S(1)}, f32[72,2,1024]{2,0,1:T(8,128)S(1)}, u32[]{:S(2)}, u32[]{:S(2)}) %collective-permute-start.4) | collective-permute-done | bytes 589856 | tf_op jit(solution)/shard_map/ppermute | solution.py:21
  102.3 4.1 collective-permute-done.5
  106.5 3.5 pad_maximum_fusion.6
  110.1 5.8 fusion.112
  115.9 13.2 %multiply_multiply_fusion.5 = (f32[72,18,1024]{2,0,1:T(8,128)}, f32[72,18,1024]{2,0,1:T(8,128)}) fusion(f32[72,18,1023]{2,0,1:T(8,128)} %get-tuple-element.18, f32[72,2,1024]{2,0,1:T(8,128)S(1)} %collective-permute-done.5, f32[72,16,1024]{2,0,1:T(8,128)S(1)} %bitcast.124, f32[72,2,1024]{2,0,1:T(8,128)S(1)} %collective-permute-done.4, ...), kind=kLoop, calls=%fused_computation.98 | loop fusion | flops 39813120 | bytes 32503680 | tf_op jit(solution)/shard_map/mul | solution.py:53
  129.0 1.3 slice.459
  130.3 6.5 slice.458
  136.8 6.4 fusion.2
  143.3 6.0 fusion.6
  149.6 4.2 fusion.72
  153.8 6.1 all-to-all-start
  160.7 4.3 scatter_custom_fusion
  165.0 81.7 %all-to-all-done = f32[72,16,1024]{2,0,1:T(8,128)} async-done(((f32[72,16,1024]{2,0,1:T(8,128)}), f32[72,16,1024]{2,0,1:T(8,128)}, u32[]{:S(2)}, u32[]{:S(2)}) %all-to-all-start) | async-done | bytes 4718624 | tf_op jit(solution)/shard_map/all_to_all | solution.py:116
  246.7 6.0 copy.42
  252.8 42.3 %fusion.120 = f32[1024,1152]{1,0:T(8,128)} fusion(f32[1152,1024]{1,0:T(8,128)} %bitcast.10, f32[1152,1152]{1,0:T(8,128)} %all-gather.3.cloned.1.call-done), kind=kOutput, calls=%fused_computation.245 | convolution fusion | flops 16307453952 | bytes 14745600 | tf_op jit(solution)/shard_map/dot_general | solution.py:119
  295.1 44.7 %fusion.93 = f32[1152,1,1024]{0,2,1:T(8,128)} fusion(f32[1152,1024]{0,1:T(8,128)} %copy.42, f32[1152,1024]{1,0:T(8,128)} %bitcast.10, f32[1152,1152]{1,0:T(8,128)} %all-gather.5.cloned.1.call-done, f32[1024,1152]{1,0:T(8,128)} %fusion.120, f32[1024]{0:T(1024)S(1)} %fusion.103, f32[1152]{0:T(1024)S(1)} %copy-done.10), kind=kOutput, calls=%fused_computation.179 | convolution fusion | flops 16326328320 | bytes 24191488 | tf_op jit(solution)/shard_map/dot_general | solution.py:122
  339.8 11.5 %copy.43 = f32[1152,1,1024]{2,1,0:T(1,128)} copy(f32[1152,1,1024]{0,2,1:T(8,128)} %fusion.93) | data formatting | bytes 9437184 | tf_op jit(solution)/shard_map/reshape | solution.py:130
  351.3 125.2 %all_to_all.66 = f32[1152,1,1024]{2,1,0:T(1,128)S(1)} all-to-all(f32[1152,1,1024]{2,1,0:T(1,128)} %copy.43), channel_id=1, replica_groups=mesh['lat'=2,'comp'=16] {'comp'}, dimensions={0} | all-to-all | bytes 9437184 | tf_op jit(solution)/shard_map/all_to_all | solution.py:129
  476.5 1.1 copy.50
  477.8 1.4 collective-permute-start.6
  479.2 1.5 collective-permute-start.7
  480.7 12.2 %collective-permute-done.6 = f32[72,2,1024]{2,0,1:T(8,128)S(1)} collective-permute-done((f32[72,2,1024]{2,0,1:T(8,128)S(1)}, f32[72,2,1024]{2,0,1:T(8,128)S(1)}, u32[]{:S(2)}, u32[]{:S(2)}) %collective-permute-start.6) | collective-permute-done | bytes 589856 | tf_op jit(solution)/shard_map/ppermute | solution.py:21
  492.9 4.1 collective-permute-done.7
  497.0 3.1 pad_maximum_fusion.7
  500.1 9.6 %fusion.111 = (f32[72,18,1023]{2,0,1:T(8,128)}, f32[72,18,1023]{2,0,1:T(8,128)}) fusion(f32[72,20,1024]{2,0,1:T(8,128)} %pad_maximum_fusion.7), kind=kLoop, calls=%fused_computation.236 | loop fusion | bytes 21212928 | tf_op jit(solution)/shard_map/jit(_roll_static)/slice | solution.py:51
  509.7 12.9 %multiply_multiply_fusion.3 = (f32[72,18,1024]{2,0,1:T(8,128)S(1)}, f32[72,18,1024]{2,0,1:T(8,128)}) fusion(f32[72,18,1023]{2,0,1:T(8,128)} %get-tuple-element.16, f32[72,2,1024]{2,0,1:T(8,128)S(1)} %collective-permute-done.7, f32[72,16,1024]{2,0,1:T(8,128)S(1)} %bitcast.127, f32[72,2,1024]{2,0,1:T(8,128)S(1)} %collective-permute-done.6, ...), kind=kLoop, calls=%fused_computation.96 | loop fusion | flops 39813120 | bytes 32503680 | tf_op jit(solution)/shard_map/mul | solution.py:53
  522.8 3.7 slice.477
  526.5 6.5 fusion.1
  533.2 5.9 fusion.5
  539.1 2.8 fusion.69
  542.0 1.5 collective-permute-start.8
  543.5 1.7 collective-permute-start.9
  545.2 10.9 %collective-permute-done.8 = f32[72,2,1024]{2,0,1:T(8,128)S(1)} collective-permute-done((f32[72,2,1024]{2,0,1:T(8,128)S(1)}, f32[72,2,1024]{2,0,1:T(8,128)S(1)}, u32[]{:S(2)}, u32[]{:S(2)}) %collective-permute-start.8) | collective-permute-done | bytes 589856 | tf_op jit(solution)/shard_map/ppermute | solution.py:21
  556.2 4.1 collective-permute-done.9
  561.3 5.9 fusion.110
  567.2 13.1 %multiply_multiply_fusion.1 = (f32[72,18,1024]{2,0,1:T(8,128)}, f32[72,18,1024]{2,0,1:T(8,128)}) fusion(f32[72,18,1023]{2,0,1:T(8,128)} %get-tuple-element.14, f32[72,2,1024]{2,0,1:T(8,128)S(1)} %collective-permute-done.9, f32[72,16,1024]{2,0,1:T(8,128)S(1)} %fusion.69, f32[72,2,1024]{2,0,1:T(8,128)S(1)} %collective-permute-done.8, ...), kind=kLoop, calls=%fused_computation.94 | loop fusion | flops 39813120 | bytes 32503680 | tf_op jit(solution)/shard_map/mul | solution.py:53
  580.3 1.3 slice.496
  581.6 6.6 slice.495
  588.1 6.5 fusion
  594.9 5.9 fusion.4
  600.8 2.9 fusion.66
  603.6 107.8 %all_to_all.67 = f32[72,16,1024]{2,0,1:T(8,128)} all-to-all(f32[72,16,1024]{2,0,1:T(8,128)S(1)} %fusion.66), channel_id=1, replica_groups=mesh['lat'=2,'comp'=16] {'comp'}, dimensions={1} | all-to-all | bytes 9437184 | tf_op jit(solution)/shard_map/all_to_all | solution.py:116
  711.5 6.1 copy.47
  717.6 40.9 %fusion.121 = f32[1024,1152]{1,0:T(8,128)S(1)} fusion(f32[1152,1024]{1,0:T(8,128)} %bitcast.144, f32[1152,1152]{1,0:T(8,128)} %all-gather.3.cloned.1.call-done), kind=kOutput, calls=%fused_computation.246 | convolution fusion | flops 16307453952 | bytes 14745600 | tf_op jit(solution)/shard_map/dot_general | solution.py:119
  758.5 56.3 %fusion.83 = f32[1152,1,1024]{0,2,1:T(8,128)} fusion(f32[1152,1024]{0,1:T(8,128)S(1)} %copy-done.2, f32[1152,1024]{1,0:T(8,128)S(1)} %bitcast.147, f32[1152,1152]{1,0:T(8,128)} %all-gather.5.cloned.1.call-done, f32[1024,1152]{1,0:T(8,128)S(1)} %fusion.121, f32[1024]{0:T(1024)S(1)} %fusion.103, f32[1152]{0:T(1024)S(1)} %copy-done.11), kind=kOutput, calls=%fused_computation.164 | convolution fusion | flops 16326328320 | bytes 24191488 | tf_op jit(solution)/shard_map/dot_general | solution.py:122
  814.9 11.5 %copy.48 = f32[1152,1,1024]{2,1,0:T(1,128)} copy(f32[1152,1,1024]{0,2,1:T(8,128)} %fusion.83) | data formatting | bytes 9437184 | tf_op jit(solution)/shard_map/reshape | solution.py:130
  826.4 108.8 %all_to_all.68 = f32[1152,1,1024]{2,1,0:T(1,128)S(1)} all-to-all(f32[1152,1,1024]{2,1,0:T(1,128)} %copy.48), channel_id=1, replica_groups=mesh['lat'=2,'comp'=16] {'comp'}, dimensions={0} | all-to-all | bytes 9437184 | tf_op jit(solution)/shard_map/all_to_all | solution.py:129
  936.4 4.9 copy.49
  (90 shorter events, 9.1 us)
Async XLA Ops:
  6.5 26.4 %copy-start.8 = (f32[2,16,1024]{2,1,0:T(8,128)S(1)}, f32[2,16,1024]{2,1,0:T(8,128)}, u32[]{:S(2)}) copy-start(f32[2,16,1024]{2,1,0:T(8,128)} %param.12) | copy-start | bytes 393220
  6.5 246.2 %all-gather.3.cloned.1.call-start = ((), (), s32[]{:S(2)}) async-start(), calls=%async_computation.4 | async-start | bytes 7962624 | tf_op jit(solution)/shard_map/all_gather | solution.py:107
  9.8 23.5 %collective-permute-start.2 = (f32[72,2,1024]{2,0,1:T(8,128)S(1)}, f32[72,2,1024]{2,0,1:T(8,128)S(1)}, u32[]{:S(2)}, u32[]{:S(2)}) collective-permute-start(f32[72,2,1024]{2,0,1:T(8,128)S(1)} %copy.56), channel_id=1, source_target_pairs={{0,16},{1,17},{2,18},{3,19},{4,20},{5,21},{6,22},{7,23},{8,24},{9,... | collective-permute-start | bytes 1769480 | tf_op jit(solution)/shard_map/ppermute | solution.py:21
  14.9 26.9 %collective-permute-start.3 = (f32[72,2,1024]{2,0,1:T(8,128)S(1)}, f32[72,2,1024]{2,0,1:T(8,128)S(1)}, u32[]{:S(2)}, u32[]{:S(2)}) collective-permute-start(f32[72,2,1024]{2,0,1:T(8,128)S(1)} %copy.57), channel_id=1, source_target_pairs={{16,0},{17,1},{18,2},{19,3},{20,4},{21,5},{22,6},{23,7},{24,8},{25... | collective-permute-start | bytes 1769480 | tf_op jit(solution)/shard_map/ppermute | solution.py:23
  17.0 132.5 %copy-start.5 = (f32[16,1024]{1,0:T(8,128)}, f32[16,1024]{1,0:T(8,128)S(1)}, u32[]{:S(2)}) copy-start(f32[16,1024]{1,0:T(8,128)S(1)} %get-tuple-element.42) | copy-start | bytes 196612
  18.8 14.2 %collective-permute-start.1 = (f32[4,3,1024]{2,1,0:T(4,128)S(1)}, f32[4,3,1024]{2,1,0:T(4,128)S(1)}, u32[]{:S(2)}, u32[]{:S(2)}) collective-permute-start(f32[4,3,1024]{2,1,0:T(4,128)S(1)} %get-tuple-element.41), channel_id=1, source_target_pairs={{16,0},{17,1},{18,2},{19,3},{20,4},{21,5},{22,6},{23,7},{24,8},{25... | collective-permute-start | bytes 147464 | tf_op jit(solution)/shard_map/ppermute | solution.py:23
  20.1 12.9 %collective-permute-start = (f32[4,3,1024]{2,1,0:T(4,128)S(1)}, f32[4,3,1024]{2,1,0:T(4,128)S(1)}, u32[]{:S(2)}, u32[]{:S(2)}) collective-permute-start(f32[4,3,1024]{2,1,0:T(4,128)S(1)} %get-tuple-element.40), channel_id=1, source_target_pairs={{0,16},{1,17},{2,18},{3,19},{4,20},{5,21},{6,22},{7,23},{8,24},{9,... | collective-permute-start | bytes 147464 | tf_op jit(solution)/shard_map/ppermute | solution.py:21
  33.2 493.3 %copy-start.3 = (f32[18,1024]{1,0:T(8,128)}, f32[18,1024]{1,0:T(8,128)S(1)}, u32[]{:S(2)}) copy-start(f32[18,1024]{1,0:T(8,128)S(1)} %fusion.102) | copy-start | bytes 221188
  41.9 5.8 copy-start.1
  62.3 3.9 slice-start.8
  62.4 3.8 slice-start.9
  87.1 2.2 copy-start
  89.4 13.0 %collective-permute-start.4 = (f32[72,2,1024]{2,0,1:T(8,128)S(1)}, f32[72,2,1024]{2,0,1:T(8,128)S(1)}, u32[]{:S(2)}, u32[]{:S(2)}) collective-permute-start(f32[72,2,1024]{2,0,1:T(8,128)S(1)} %get-tuple-element.28), channel_id=1, source_target_pairs={{0,16},{1,17},{2,18},{3,19},{4,20},{5,21},{6,22},{7,23},{8,24},{9,... | collective-permute-start | bytes 1769480 | tf_op jit(solution)/shard_map/ppermute | solution.py:21
  90.9 15.6 %collective-permute-start.5 = (f32[72,2,1024]{2,0,1:T(8,128)S(1)}, f32[72,2,1024]{2,0,1:T(8,128)S(1)}, u32[]{:S(2)}, u32[]{:S(2)}) collective-permute-start(f32[72,2,1024]{2,0,1:T(8,128)S(1)} %get-tuple-element.27), channel_id=1, source_target_pairs={{16,0},{17,1},{18,2},{19,3},{20,4},{21,5},{22,6},{23,7},{24,8},{25... | collective-permute-start | bytes 1769480 | tf_op jit(solution)/shard_map/ppermute | solution.py:23
  106.5 9.4 slice-start
  110.1 5.8 slice-start.1
  129.0 7.8 slice-start.6
  130.3 6.5 slice-start.7
  153.8 6.9 copy-start.9
  153.8 92.9 %all-to-all-start = ((f32[72,16,1024]{2,0,1:T(8,128)}), f32[72,16,1024]{2,0,1:T(8,128)}, u32[]{:S(2)}, u32[]{:S(2)}) async-start(f32[72,16,1024]{2,0,1:T(8,128)} %fusion.72), calls=%async_computation | async-start | bytes 9437184 | tf_op jit(solution)/shard_map/all_to_all | solution.py:116
  159.9 135.2 %all-gather.5.cloned.1.call-start = ((), (), s32[]{:S(2)}) async-start(), calls=%async_computation.5 | async-start | bytes 7962624 | tf_op jit(solution)/shard_map/all_gather | solution.py:108
  252.7 42.3 %copy-start.10 = (f32[1152]{0:T(1024)S(1)}, f32[1152]{0:T(1024)}, u32[]{:S(2)}) copy-start(f32[1152]{0:T(1024)} %param.11) | copy-start | bytes 13828
  477.8 15.1 %collective-permute-start.6 = (f32[72,2,1024]{2,0,1:T(8,128)S(1)}, f32[72,2,1024]{2,0,1:T(8,128)S(1)}, u32[]{:S(2)}, u32[]{:S(2)}) collective-permute-start(f32[72,2,1024]{2,0,1:T(8,128)S(1)} %get-tuple-element.26), channel_id=1, source_target_pairs={{0,16},{1,17},{2,18},{3,19},{4,20},{5,21},{6,22},{7,23},{8,24},{9,... | collective-permute-start | bytes 1769480 | tf_op jit(solution)/shard_map/ppermute | solution.py:21
  479.2 17.8 %collective-permute-start.7 = (f32[72,2,1024]{2,0,1:T(8,128)S(1)}, f32[72,2,1024]{2,0,1:T(8,128)S(1)}, u32[]{:S(2)}, u32[]{:S(2)}) collective-permute-start(f32[72,2,1024]{2,0,1:T(8,128)S(1)} %get-tuple-element.25), channel_id=1, source_target_pairs={{16,0},{17,1},{18,2},{19,3},{20,4},{21,5},{22,6},{23,7},{24,8},{25... | collective-permute-start | bytes 1769480 | tf_op jit(solution)/shard_map/ppermute | solution.py:23
  522.7 3.8 slice-start.2
  522.8 3.7 slice-start.3
  533.2 5.9 copy-start.6
  542.0 14.1 %collective-permute-start.8 = (f32[72,2,1024]{2,0,1:T(8,128)S(1)}, f32[72,2,1024]{2,0,1:T(8,128)S(1)}, u32[]{:S(2)}, u32[]{:S(2)}) collective-permute-start(f32[72,2,1024]{2,0,1:T(8,128)S(1)} %get-tuple-element.24), channel_id=1, source_target_pairs={{0,16},{1,17},{2,18},{3,19},{4,20},{5,21},{6,22},{7,23},{8,24},{9,... | collective-permute-start | bytes 1769480 | tf_op jit(solution)/shard_map/ppermute | solution.py:21
  543.5 16.8 %collective-permute-start.9 = (f32[72,2,1024]{2,0,1:T(8,128)S(1)}, f32[72,2,1024]{2,0,1:T(8,128)S(1)}, u32[]{:S(2)}, u32[]{:S(2)}) collective-permute-start(f32[72,2,1024]{2,0,1:T(8,128)S(1)} %get-tuple-element.23), channel_id=1, source_target_pairs={{16,0},{17,1},{18,2},{19,3},{20,4},{21,5},{22,6},{23,7},{24,8},{25... | collective-permute-start | bytes 1769480 | tf_op jit(solution)/shard_map/ppermute | solution.py:23
  580.3 7.9 slice-start.4
  581.5 6.6 slice-start.5
  581.6 6.6 copy-start.4
  594.8 5.9 copy-start.7
  711.5 47.0 %slice-start.10 = ((s8[4718592]{0:T(1024)(128)(4,1)}), s8[524288]{0:T(1024)(128)(4,1)S(1)}, s32[]{:S(2)}) async-start(s8[4718592]{0:T(1024)(128)(4,1)} %bitcast.145), calls=%async_computation.16 | async-start | bytes 1048576
  717.6 40.9 %slice-start.11 = ((s8[4718592]{0:T(1024)(128)(4,1)}), s8[4194304]{0:T(1024)(128)(4,1)S(1)}, s32[]{:S(2)}) async-start(s8[4718592]{0:T(1024)(128)(4,1)} %bitcast.145), calls=%async_computation.17 | async-start | bytes 8388608
  717.6 40.9 %copy-start.2 = (f32[1152,1024]{0,1:T(8,128)S(1)}, f32[1152,1024]{0,1:T(8,128)}, u32[]{:S(2)}) copy-start(f32[1152,1024]{0,1:T(8,128)} %copy.47) | copy-start | bytes 14155780
  717.6 40.9 %copy-start.11 = (f32[1152]{0:T(1024)S(1)}, f32[1152]{0:T(1024)}, u32[]{:S(2)}) copy-start(f32[1152]{0:T(1024)} %param.11) | copy-start | bytes 13828
Sparse Core Ops, SparseCore 0:
  92.3 71.6 all-gather.2
  165.6 69.2 all-gather.4
where the time goes:
time: 956 us; the launch traced here: 948 us
  blocking collectives  342 us (36%)
  matrix products  184 us (19%)
  waiting for transfers between devices  136 us (14%)
  other arithmetic  132 us (14%)
  local copies, waits for them, and re-layouts  113 us (12%)
  starting transfers between devices  27.1 us (3%)
  between operations  14.2 us (1%)
    all_to_all x2, blocking collectives, body(): lax.all_to_all(updated.reshape(K, 1, points), 'comp', split_axis=0, conca...  234 us
    all_to_all x1, blocking collectives, body(): lax.all_to_all(spread, 'comp', split_axis=1, concat_axis=0, tiled=True)  108 us
    dot_general x2, matrix products, body(): jnp.dot(minus_full, gathered, precision=lax.Precision.HIGHEST, preferred_...  101 us
    dot_general x2, matrix products, body(): jnp.dot(plus_full, gathered, precision=lax.Precision.HIGHEST, preferred_e...  83.2 us
    all_to_all x1, waiting for transfers between devices, body(): lax.all_to_all(spread, 'comp', split_axis=1, concat_axis=0, tiled=True)  81.7 us
    mul x4, other arithmetic, advect(): slope_x = flagged * minmod(east - centre, centre - west)  53.5 us
    ppermute x5, waiting for transfers between devices, padded_2(): lax.ppermute(tail, axis, [(i, (i + 1) % count) for i in range(ends)])  33.2 us
    slice x5, local copies, waits for them, and re-layouts, advect(): east = jnp.roll(centre, -1, axis=2)  27.2 us
  transfers between devices with their start and end apart: 13, of which 8 were waited for; matrix products, arithmetic and copies ran while one was open for 12% of the time, Pallas kernels for 0%

commit v1 on v0

v1 whole, which is shorter than its diff:
```python
import functools

import jax
import jax.numpy as jnp
from jax import lax
from jax.experimental import pallas as pl
from jax.experimental.pallas import tpu as pltpu
from jax.sharding import PartitionSpec as P

ND = 36
NF = 32
OUTER = 2
SUB = 2
HALO = 2 * SUB
LANES = 128
BOTH = ("lat", "comp")


def speeds(index):
    direction = (index // NF).astype(jnp.float32)
    frequency = (index % NF).astype(jnp.float32)
    angle_dir = 2.0 * jnp.pi * (direction + 0.5) / ND
    magnitude = 0.35 * (0.5 + 0.5 * frequency / (NF - 1))
    return (magnitude * jnp.cos(angle_dir))[None, :], (magnitude * jnp.sin(angle_dir))[None, :]


def minmod(first, second):
    return jnp.maximum(jnp.minimum(first, second), 0.0) + jnp.minimum(jnp.maximum(first, second), 0.0)


def upwind(face, low, low_slope, high, high_slope):
    half = 0.5 - 0.5 * jnp.abs(face)
    return face * jnp.where(face >= 0.0, low + half * low_slope, high - half * high_slope)


def advect_kernel(
    cx_ref, cy_ref, uf_ref, vf_ref, flag_ref, sea_ref, field_ref, left_ref, right_ref, out_ref, first, second
):
    rows, lons, lanes = field_ref.shape
    wide = lons + 2 * HALO
    zero = jnp.zeros((wide, lanes), jnp.float32)
    first[:rows, :HALO, :] = left_ref[...]
    first[:rows, HALO : HALO + lons, :] = field_ref[...]
    first[:rows, HALO + lons :, :] = right_ref[...]
    for extra in range(2):
        first[rows + extra] = zero
        second[rows + extra] = zero
    speed_x = cx_ref[...]
    speed_y = cy_ref[...]

    def substep(source, store):
        top = source[0]
        below = source[1]
        step = below - top
        slope = flag_ref[0] * minmod(step, top)
        flux = upwind(speed_y + vf_ref[0], zero, zero, top, slope)

        def row(r, carry):
            here, south, step, slope, flux = carry
            beyond = source[r + 2]
            next_step = beyond - south
            next_slope = flag_ref[r + 1] * minmod(next_step, step)
            next_flux = upwind(speed_y + vf_ref[r + 1], here, slope, south, next_slope)
            east = pltpu.roll(here, wide - 1, 0)
            forward = east - here
            slope_x = flag_ref[r] * minmod(forward, pltpu.roll(forward, 1, 0))
            flux_x = upwind(
                speed_x + uf_ref[r], here, slope_x, east, pltpu.roll(slope_x, wide - 1, 0)
            )
            change_x = flux_x - pltpu.roll(flux_x, 1, 0)
            store(r, sea_ref[r] * (here - change_x - (next_flux - flux)))
            return south, beyond, next_step, next_slope, next_flux

        lax.fori_loop(0, rows, row, (top, below, step, slope, flux), unroll=2)

    def keep_second(r, value):
        second[r] = value

    def keep_out(r, value):
        out_ref[r] = value[HALO : HALO + lons]

    substep(first, keep_second)
    substep(second, keep_out)


def advect(field, left, right, fixed):
    speed_x, speed_y, face_u, face_v, flag, sea = fixed
    rows, lons, comps = field.shape
    wide = lons + 2 * HALO
    column = lambda height: pl.BlockSpec((rows, height, LANES), lambda k: (0, 0, k))
    whole = lambda array: pl.BlockSpec(array.shape, lambda k: (0, 0, 0))
    return pl.pallas_call(
        advect_kernel,
        grid=(comps // LANES,),
        out_shape=jax.ShapeDtypeStruct(field.shape, jnp.float32),
        in_specs=[
            pl.BlockSpec((1, LANES), lambda k: (0, k)),
            pl.BlockSpec((1, LANES), lambda k: (0, k)),
            whole(face_u),
            whole(face_v),
            whole(flag),
            whole(sea),
            column(lons),
            column(HALO),
            column(HALO),
        ],
        out_specs=column(lons),
        scratch_shapes=[pltpu.VMEM((rows + 2, wide, LANES), jnp.float32)] * 2,
        compiler_params=pltpu.CompilerParams(vmem_limit_bytes=40 * 2**20),
        name="advect",
    )(speed_x, speed_y, face_u, face_v, flag, sea, field, left, right)


def source_kernel(field_ref, high_ref, low_ref, gain_ref, keep_ref, out_ref):
    comps = field_ref.shape[1]
    field = field_ref[...]
    field_high = field.astype(jnp.bfloat16)
    field_low = (field - field_high.astype(jnp.float32)).astype(jnp.bfloat16)

    def product(start):
        dims = (((1,), (1,)), ((), ()))
        dot = functools.partial(lax.dot_general, dimension_numbers=dims, preferred_element_type=jnp.float32)
        high = high_ref[start : start + comps, :]
        low = low_ref[start : start + comps, :]
        return dot(field_high, low) + dot(field_low, high) + dot(field_high, high)

    plus = product(0)
    minus = product(comps)
    gain = gain_ref[...]
    forcing = field * (field * (plus + minus) - 2.0 * plus * minus)
    update = gain * forcing / (1.0 + gain * (plus * plus + minus * minus))
    out_ref[...] = (field + update) * keep_ref[...]


def source(field, high, low, gain, keep):
    points, comps = field.shape
    tile = min(256, points)
    return pl.pallas_call(
        source_kernel,
        grid=(points // tile,),
        out_shape=jax.ShapeDtypeStruct(field.shape, jnp.float32),
        in_specs=[
            pl.BlockSpec((tile, comps), lambda p: (p, 0)),
            pl.BlockSpec(high.shape, lambda p: (0, 0)),
            pl.BlockSpec(low.shape, lambda p: (0, 0)),
            pl.BlockSpec((1, comps), lambda p: (0, 0)),
            pl.BlockSpec((tile, 1), lambda p: (p, 0)),
        ],
        out_specs=pl.BlockSpec((tile, comps), lambda p: (p, 0)),
        compiler_params=pltpu.CompilerParams(vmem_limit_bytes=56 * 2**20),
        name="source",
    )(field, high, low, gain, keep)


def body(
    spectrum, interp_plus, interp_minus, source_gain, current, sea_mask, limiter_flags, ice_cells
):
    bands = lax.axis_size("lat")
    ranks = lax.axis_size("comp")
    count = bands * ranks
    local_k, band_rows, lon_count = spectrum.shape
    comps = local_k * ranks
    rows = band_rows * bands
    lons = lon_count // count
    lat_rank = lax.axis_index("lat")
    comp_rank = lax.axis_index("comp")

    order = [
        band * ranks + (rank if band % 2 == 0 else ranks - 1 - rank)
        for band in range(bands)
        for rank in range(ranks)
    ]
    block = lat_rank * ranks + jnp.where(lat_rank % 2 == 0, comp_rank, ranks - 1 - comp_rank)

    def snake(blocks):
        parts = [
            blocks[band * ranks : (band + 1) * ranks] for band in range(bands)
        ]
        return jnp.concatenate([part if band % 2 == 0 else part[::-1] for band, part in enumerate(parts)])

    spread = snake(spectrum.reshape(local_k, band_rows, count, lons).transpose(2, 0, 1, 3))
    spread = spread.reshape(count, local_k, band_rows * lons)
    gathered = lax.all_to_all(spread, BOTH, split_axis=0, concat_axis=0, tiled=True)
    field = gathered.reshape(bands, comps, band_rows * lons).transpose(0, 2, 1)
    field = field.reshape(rows, lons, comps)

    statics = jnp.stack(
        [current[0], current[1], limiter_flags.astype(jnp.float32), sea_mask.astype(jnp.float32)]
    )
    statics = lax.all_gather(statics, "lat", axis=1, tiled=True)
    wide = lons + 2 * HALO
    ring = jnp.concatenate([statics[:, :, -HALO:], statics, statics[:, :, : HALO + 1]], axis=2)
    window = lax.dynamic_slice(ring, (0, 0, block * lons), (4, rows, wide + 1))
    drift_x, drift_y, flag, sea = window
    lanes = lambda plane: jnp.broadcast_to(plane[:, :, None], plane.shape + (LANES,))
    face_u = lanes(0.5 * (drift_x[:, :wide] + drift_x[:, 1:]))
    edged = jnp.pad(drift_y[:, :wide], ((1, 1), (0, 0)))
    face_v = lanes(0.5 * (edged[:-1] + edged[1:]))
    flag = lanes(jnp.pad(flag[:, :wide], ((0, 1), (0, 0))))
    sea = lanes(sea[:, :wide])
    speed_x, speed_y = speeds(jnp.arange(comps, dtype=jnp.int32))
    fixed = (speed_x, speed_y, face_u, face_v, flag, sea)

    cell = (
        jnp.arange(rows, dtype=jnp.int32)[:, None] * lon_count
        + block * lons
        + jnp.arange(lons, dtype=jnp.int32)[None, :]
    ).reshape(rows * lons)
    iced = jnp.any(cell[:, None] == ice_cells[None, :], axis=1)
    keep = jnp.where(iced, 1.0 - 0.6 * 1.0, 1.0).astype(jnp.float32)[:, None]

    weights = jnp.concatenate(
        [
            lax.all_gather(interp_plus, "lat", axis=0, tiled=True),
            lax.all_gather(interp_minus, "lat", axis=0, tiled=True),
        ]
    )
    rounded = lax.reduce_precision(weights, 8, 7)
    high = rounded.astype(jnp.bfloat16)
    low = (weights - rounded).astype(jnp.bfloat16)
    gain = source_gain[None, :]

    eastward = [(order[b], order[(b + 1) % count]) for b in range(count)]
    westward = [(order[(b + 1) % count], order[b]) for b in range(count)]
    for outer_step in range(OUTER):
        left = lax.ppermute(field[:, lons - HALO :], BOTH, eastward)
        right = lax.ppermute(field[:, :HALO], BOTH, westward)
        field = advect(field, left, right, fixed)
        field = source(field.reshape(rows * lons, comps), high, low, gain, keep)
        field = field.reshape(rows, lons, comps)

    spread = field.reshape(bands, band_rows * lons, comps).transpose(0, 2, 1)
    spread = spread.reshape(count, local_k, band_rows * lons)
    gathered = lax.all_to_all(spread, BOTH, split_axis=0, concat_axis=0, tiled=True)
    blocks = snake(gathered).reshape(count, local_k, band_rows, lons)
    return blocks.transpose(1, 2, 0, 3).reshape(local_k, band_rows, lon_count)


def solution(mesh):
    placed = (
        P("comp", "lat", None),
        P("lat", None),
        P("lat", None),
        P(),
        P(None, "lat", None),
        P("lat", None),
        P("lat", None),
        P(),
    )
    return jax.shard_map(
        body, mesh=mesh, in_specs=placed, out_specs=P("comp", "lat", None), check_vma=False
    )
```

time: 956 us -> 518 us (0.54)
  matrix products: 184 us -> 0 us
  blocking collectives: 342 us -> 172 us
  other arithmetic: 132 us -> 20.8 us
  Pallas kernels: 0 us -> 100 us
  waiting for transfers between devices: 136 us -> 95.4 us
  local copies, waits for them, and re-layouts: 113 us -> 100 us
  starting transfers between devices: 27.1 us -> 14.6 us
    all_to_all x3 -> x1, blocking collectives: 342 us -> 115 us  [body(): lax.all_to_all(spread, BOTH, split_axis=0, concat_axis=0, tiled=True)]
    dot_general x4 -> x0, matrix products: 184 us -> none  [the longest x2 101 us: body(): jnp.dot(minus_full, gathered, precision=lax.Precision.HIGHEST, preferred_...]
    pallas_call x0 -> x4, Pallas kernels: none -> 100 us  [the longest x2 54.4 us: source(): pl.pallas_call(source_kernel, grid=(points // tile,), out_shape=jax.Shape...]
    all_to_all x1, waiting for transfers between devices: 81.7 us -> 0.01 us  [body(): lax.all_to_all(spread, BOTH, split_axis=0, concat_axis=0, tiled=True)]
    all_gather x1, waiting for transfers between devices: 0.02 us -> 76.7 us  [body(): lax.all_gather(interp_minus, 'lat', axis=0, tiled=True)]
    mul x8 -> x2, other arithmetic: 70.5 us -> 0.08 us  [the longest x1 0.07 us: body(): face_u = lanes(0.5 * (drift_x[:, :wide] + drift_x[:, 1:]))]
    all_gather x0 -> x1, blocking collectives: none -> 57.7 us  [body(): statics = lax.all_gather(statics, 'lat', axis=1, tiled=True)]
    select_n x9 -> x1, other arithmetic: 50.8 us -> 0.01 us  [body(): keep = jnp.where(iced, 1.0 - 0.6 * 1.0, 1.0).astype(jnp.float32)[:, None]]
  transfers between devices with their start and end apart: 13 -> 7, of which waited for: 8 -> 5; matrix products, arithmetic and copies ran while one was open for 12% -> 12% of each run, Pallas kernels for 0% -> 0%
where the time goes in v1:
time: 518 us; the launch traced here: 517 us
  blocking collectives  172 us (33%)
  local copies, waits for them, and re-layouts  100 us (19%)
  Pallas kernels  100 us (19%)
  waiting for transfers between devices  95.4 us (18%)
  other arithmetic  20.8 us (4%)
  starting transfers between devices  14.6 us (3%)
  between operations  13.6 us (3%)
    all_to_all x1, blocking collectives, body(): lax.all_to_all(spread, BOTH, split_axis=0, concat_axis=0, tiled=True)  115 us
    all_gather x1, waiting for transfers between devices, body(): lax.all_gather(interp_minus, 'lat', axis=0, tiled=True)  76.7 us
    all_gather x1, blocking collectives, body(): statics = lax.all_gather(statics, 'lat', axis=1, tiled=True)  57.7 us
    pallas_call x2, Pallas kernels, source(): pl.pallas_call(source_kernel, grid=(points // tile,), out_shape=jax.Shape...  54.4 us
    pallas_call x2, Pallas kernels, advect(): pl.pallas_call(advect_kernel, grid=(comps // LANES,), out_shape=jax.Shape...  45.7 us
    unnamed x20, local copies, waits for them, and re-layouts  22.1 us
    concatenate x2, local copies, waits for them, and re-layouts, snake(): jnp.concatenate([part if band % 2 == 0 else part[::-1] for band, part in...  12.2 us
    slice x2, local copies, waits for them, and re-layouts, snake(): parts = [blocks[band * ranks:(band + 1) * ranks] for band in range(bands)]  11.1 us
  transfers between devices with their start and end apart: 7, of which 5 were waited for; matrix products, arithmetic and copies ran while one was open for 12% of the time, Pallas kernels for 0%

profile of v1, /device:TPU:0, one launch (start us, length us, event | category | flops | bytes accessed | tf_op | source)
XLA Modules:
  0.0 517.4 jit_solution(15047019334414877053)
XLA Ops:
  6.5 0.0 all-gather.3.cloned.1.call-start
  6.5 0.7 all-gather.3.cloned.1.call-update
  7.3 7.8 %copy.29 = f32[72,16,1024]{0,2,1:T(8,128)} copy(f32[72,16,1024]{2,1,0:T(8,128)} %param.8) | data formatting | bytes 9437184 | tf_op args[0]
  15.1 9.0 %fusion.11 = (f32[16,72,16,32]{1,3,0,2:T(8,128)}, f32[16,72,16,32]{1,3,0,2:T(8,128)}) fusion(f32[32,72,16,32]{1,3,0,2:T(8,128)} %bitcast.41), kind=kLoop, calls=%fused_computation.38 | loop fusion | bytes 9437184 | tf_op jit(solution)/shard_map/slice | solution.py:177
  24.1 5.2 %rev.6 = f32[16,72,16,32]{1,3,0,2:T(8,128)} reverse(f32[16,72,16,32]{1,3,0,2:T(8,128)} %get-tuple-element.8), dimensions={0} | reverse | bytes 4718592 | tf_op jit(solution)/shard_map/rev | solution.py:179
  29.3 5.2 %pad_maximum_fusion = f32[32,72,16,32]{1,3,0,2:T(8,128)S(1)} fusion(f32[16,72,16,32]{1,3,0,2:T(8,128)} %rev.6, f32[16,72,16,32]{1,3,0,2:T(8,128)} %get-tuple-element.7), kind=kLoop, calls=%fused_computation.3 | loop fusion | flops 1179648 | bytes 9437184 | tf_op jit(solution)/shard_map/concatenate | solution.py:179
  34.5 4.7 copy.30
  39.2 8.0 %copy.31 = f32[32,72,512]{2,1,0:T(8,128)} copy(f32[32,72,512]{1,2,0:T(8,128)} %bitcast.42) | data formatting | bytes 9437184 | tf_op jit(solution)/shard_map/reshape | solution.py:182
  47.2 0.0 copy-start.8
  47.2 7.7 %all-to-all-start = ((f32[32,72,512]{2,1,0:T(8,128)}), f32[32,72,512]{2,1,0:T(8,128)}, u32[]{:S(2)}, u32[]{:S(2)}) async-start(f32[32,72,512]{2,1,0:T(8,128)} %copy.31), calls=%async_computation | async-start | bytes 9437184 | tf_op jit(solution)/shard_map/all_to_all | solution.py:183
  55.0 0.0 all-gather.5.cloned.1.call-start
  55.0 0.7 all-gather.5.cloned.1.call-update
  55.7 0.0 copy-done.5
  55.8 57.7 %all_gather.9 = f32[4,32,1024]{2,1,0:T(8,128)S(1)} all-gather(f32[4,16,1024]{2,1,0:T(8,128)S(1)} %pad_maximum_fusion.2), channel_id=1, replica_groups=mesh['lat'=2,'comp'=16] {'lat'}, dimensions={1}, use_global_device_ids=true | all-gather | bytes 786432 | tf_op jit(solution)/shard_map/all_gather | solution.py:190
  113.5 0.1 slice.71
  113.6 0.6 broadcast_in_dim.20.gain_ref
  114.2 0.1 iota_add_fusion
  114.3 0.1 add.139
  114.4 0.7 compare_reduce_fusion
  115.1 1.0 copy.33.keep_ref
  116.1 0.3 concatenate.12
  116.4 0.1 dynamic-slice_bitcast_fusion
  116.6 0.2 sine_multiply_fusion
  116.7 0.1 fusion.3
  116.8 9.2 %all-gather.3.cloned.1.call-done = f32[1152,1152]{1,0:T(8,128)} async-done(((f32[576,1152]{1,0:T(8,128)}), f32[1152,1152]{1,0:T(8,128)}) %all-gather.3.cloned.1.call-update) | async-done | bytes 5308432 | tf_op jit(solution)/shard_map/all_gather | solution.py:214
  126.0 5.2 %constant_dynamic-update-slice_fusion.1 = f32[2304,1152]{1,0:T(8,128)} fusion(f32[1152,1152]{1,0:T(8,128)} %all-gather.3.cloned.1.call-done), kind=kLoop, calls=%fused_computation.26 | loop fusion | bytes 10616832
  131.2 76.7 %all-gather.5.cloned.1.call-done = f32[1152,1152]{1,0:T(8,128)} async-done(((f32[576,1152]{1,0:T(8,128)}), f32[1152,1152]{1,0:T(8,128)}) %all-gather.5.cloned.1.call-update) | async-done | bytes 5308432 | tf_op jit(solution)/shard_map/all_gather | solution.py:215
  208.0 5.2 %constant_dynamic-update-slice_fusion = f32[2304,1152]{1,0:T(8,128)} fusion(f32[2304,1152]{1,0:T(8,128)} %constant_dynamic-update-slice_fusion.1, f32[1152,1152]{1,0:T(8,128)} %all-gather.5.cloned.1.call-done), kind=kLoop, calls=%fused_computation.25 | loop fusion | bytes 10616832 | tf_op jit(solution)/shard_map/concatenate | solution.py:212
  213.2 0.0 all-to-all-done
  213.2 6.0 %copy.32 = f32[2,512,1152]{2,1,0:T(8,128)} copy(f32[2,512,1152]{1,2,0:T(8,128)} %bitcast.11) | data formatting | bytes 9437184 | tf_op jit(solution)/shard_map/transpose | solution.py:184
  219.3 1.8 fusion.14
  221.1 0.4 collective-permute-start.1
  221.5 0.2 collective-permute-start
  221.7 9.5 %fusion = (bf16[2304,1152]{1,0:T(8,128)(2,1)}, bf16[2304,1152]{1,0:T(8,128)(2,1)}) fusion(f32[2304,1152]{1,0:T(8,128)} %constant_dynamic-update-slice_fusion), kind=kLoop, calls=%fused_computation.2 | loop fusion | flops 10616832 | bytes 21233664 | tf_op jit(solution)/shard_map/convert_element_type | solution.py:220
  231.2 0.0 collective-permute-done.1.right_ref
  231.2 0.2 collective-permute-done.left_ref
  231.4 0.2 broadcast_in_dim.16.uf_ref
  231.6 0.2 broadcast_in_dim.19.sea_ref
  231.8 0.2 broadcast_in_dim.17.vf_ref
  232.1 0.2 broadcast_in_dim.18.flag_ref
  232.3 0.0 copy-start.1
  232.3 2.3 copy-done.1
  234.7 22.9 %advect.2 = f32[32,32,1152]{2,1,0:T(8,128)S(1)} custom-call(f32[1,1152]{1,0:T(1,128)S(1)} %get-tuple-element.22.cx_ref, f32[1,1152]{1,0:T(1,128)S(1)} %get-tuple-element.21.cy_ref, f32[32,40,128]{2,1,0:T(8,128)S(1)} %broadcast_in_dim.16.uf_ref, f32[33,40,128]{2,1,0:T(8,128)S(1)} %broadcast_in_dim.17.vf_ref, f32[33,40,128]{2,1,0:T(8,128)S(1)} %broadcast_in_dim.18.flag_ref, ...), custom_call_target="tpu_custom_call" | custom-call | tf_op jit(solution)/shard_map/advect/pallas_call | solution.py:92
  257.5 0.0 copy-start.3
  257.5 2.2 copy-done.3
  259.7 27.2 %source.2 = f32[1024,1152]{1,0:T(8,128)} custom-call(f32[1024,1152]{1,0:T(8,128)} %bitcast.40, bf16[2304,1152]{1,0:T(8,128)(2,1)} %get-tuple-element.6.high_ref, bf16[2304,1152]{1,0:T(8,128)(2,1)} %get-tuple-element.5.low_ref, f32[1,1152]{1,0:T(1,128)} %broadcast_in_dim.20.gain_ref, f32[1024,1]{1,0:T(8,128)} %copy.33.keep_ref), custom_call_target="tpu_custom_call" | custom-call | tf_op jit(solution)/shard_map/source/pallas_call | solution.py:138
  286.9 1.8 fusion.13
  288.7 1.7 collective-permute-start.3
  290.5 4.5 collective-permute-start.2
  295.0 2.9 collective-permute-done.3.right_ref
  297.9 5.0 collective-permute-done.2.left_ref
  302.9 2.3 copy-done
  305.2 22.9 %advect.3 = f32[32,32,1152]{2,1,0:T(8,128)S(1)} custom-call(f32[1,1152]{1,0:T(1,128)S(1)} %get-tuple-element.22.cx_ref, f32[1,1152]{1,0:T(1,128)S(1)} %get-tuple-element.21.cy_ref, f32[32,40,128]{2,1,0:T(8,128)S(1)} %broadcast_in_dim.16.uf_ref, f32[33,40,128]{2,1,0:T(8,128)S(1)} %broadcast_in_dim.17.vf_ref, f32[33,40,128]{2,1,0:T(8,128)S(1)} %broadcast_in_dim.18.flag_ref, ...), custom_call_target="tpu_custom_call" | custom-call | tf_op jit(solution)/shard_map/advect/pallas_call | solution.py:92
  328.1 0.0 copy-start.2
  328.1 2.2 copy-done.2
  330.3 27.2 %source.3 = f32[1024,1152]{1,0:T(8,128)} custom-call(f32[1024,1152]{1,0:T(8,128)} %bitcast.39, bf16[2304,1152]{1,0:T(8,128)(2,1)} %get-tuple-element.6.high_ref, bf16[2304,1152]{1,0:T(8,128)(2,1)} %get-tuple-element.5.low_ref, f32[1,1152]{1,0:T(1,128)} %broadcast_in_dim.20.gain_ref, f32[1024,1]{1,0:T(8,128)} %copy.33.keep_ref), custom_call_target="tpu_custom_call" | custom-call | tf_op jit(solution)/shard_map/source/pallas_call | solution.py:138
  357.5 6.0 %copy.35 = f32[2,512,1152]{1,2,0:T(8,128)} copy(f32[2,512,1152]{2,1,0:T(8,128)} %bitcast.45) | data formatting | bytes 9437184 | tf_op jit(solution)/shard_map/reshape;reshape | solution.py:232
  363.5 114.8 %all_to_all.10 = f32[32,72,512]{2,1,0:T(8,128)S(1)} all-to-all(f32[32,72,512]{2,1,0:T(8,128)} %bitcast.46), channel_id=1, replica_groups=mesh['lat'=2,'comp'=16] {'lat','comp'}, dimensions={0} | all-to-all | bytes 9437184 | tf_op jit(solution)/shard_map/all_to_all | solution.py:234
  478.3 2.1 fusion.12
  480.4 1.7 rev.7
  482.0 5.1 pad_maximum_fusion.1
  487.1 7.4 %copy.36 = f32[32,72,512]{1,2,0:T(8,128)} copy(f32[32,72,512]{2,1,0:T(8,128)} %pad_maximum_fusion.1) | data formatting | bytes 9437184 | tf_op jit(solution)/shard_map/concatenate | solution.py:179
  494.6 8.0 %copy.37 = f32[72,16,32,32]{0,3,2,1:T(8,128)} copy(f32[72,16,32,32]{0,3,1,2:T(8,128)} %bitcast.43) | data formatting | bytes 9437184 | tf_op jit(solution)/shard_map/transpose | solution.py:236
  502.6 7.9 %copy.38 = f32[72,16,1024]{2,1,0:T(8,128)} copy(f32[72,16,1024]{0,2,1:T(8,128)} %bitcast.44) | data formatting | bytes 9437184 | tf_op jit(solution)/shard_map/reshape | solution.py:236
  (16 shorter events, 0.1 us)
Async XLA Ops:
  6.5 119.5 %all-gather.3.cloned.1.call-start = ((), (), s32[]{:S(2)}) async-start(), calls=%async_computation.2 | async-start | bytes 7962624 | tf_op jit(solution)/shard_map/all_gather | solution.py:214
  47.2 8.5 %copy-start.5 = (s32[16,1024]{1,0:T(8,128)S(1)}, s32[16,1024]{1,0:T(8,128)}, u32[]{:S(2)}) copy-start(s32[16,1024]{1,0:T(8,128)} %param.13) | copy-start | bytes 196612
  47.2 8.5 %copy-start.6 = (s32[16,1024]{1,0:T(8,128)S(1)}, s32[16,1024]{1,0:T(8,128)}, u32[]{:S(2)}) copy-start(s32[16,1024]{1,0:T(8,128)} %param.14) | copy-start | bytes 196612
  47.2 8.6 %copy-start.4 = (f32[2,16,1024]{2,1,0:T(8,128)S(1)}, f32[2,16,1024]{2,1,0:T(8,128)}, u32[]{:S(2)}) copy-start(f32[2,16,1024]{2,1,0:T(8,128)} %param.12) | copy-start | bytes 393220
  47.2 66.4 %copy-start.7 = (f32[1152]{0:T(1024)S(1)}, f32[1152]{0:T(1024)}, u32[]{:S(2)}) copy-start(f32[1152]{0:T(1024)} %param.11) | copy-start | bytes 13828
  47.2 67.2 %copy-start.8 = (s32[1024]{0:T(1024)S(1)}, s32[1024]{0:T(1024)}, u32[]{:S(2)}) copy-start(s32[1024]{0:T(1024)} %param.15) | copy-start | bytes 12292
  47.2 166.0 %all-to-all-start = ((f32[32,72,512]{2,1,0:T(8,128)}), f32[32,72,512]{2,1,0:T(8,128)}, u32[]{:S(2)}, u32[]{:S(2)}) async-start(f32[32,72,512]{2,1,0:T(8,128)} %copy.31), calls=%async_computation | async-start | bytes 9437184 | tf_op jit(solution)/shard_map/all_to_all | solution.py:183
  55.0 153.0 %all-gather.5.cloned.1.call-start = ((), (), s32[]{:S(2)}) async-start(), calls=%async_computation.3 | async-start | bytes 7962624 | tf_op jit(solution)/shard_map/all_gather | solution.py:215
  221.1 10.1 %collective-permute-start.1 = (f32[32,4,1152]{2,1,0:T(4,128)S(1)}, f32[32,4,1152]{2,1,0:T(4,128)S(1)}, u32[]{:S(2)}, u32[]{:S(2)}) collective-permute-start(f32[32,4,1152]{2,1,0:T(4,128)S(1)} %get-tuple-element.13), channel_id=1, source_target_pairs={{1,0},{2,1},{3,2},{4,3},{5,4},{6,5},{7,6},{8,7},{9,8},{10,9},{11,1... | collective-permute-start | bytes 1769480 | tf_op jit(solution)/shard_map/ppermute | solution.py:227
  221.5 9.9 %collective-permute-start = (f32[32,4,1152]{2,1,0:T(4,128)S(1)}, f32[32,4,1152]{2,1,0:T(4,128)S(1)}, u32[]{:S(2)}, u32[]{:S(2)}) collective-permute-start(f32[32,4,1152]{2,1,0:T(4,128)S(1)} %get-tuple-element.14), channel_id=1, source_target_pairs={{0,1},{1,2},{2,3},{3,4},{4,5},{5,6},{6,7},{7,8},{8,9},{9,10},{10,1... | collective-permute-start | bytes 1769480 | tf_op jit(solution)/shard_map/ppermute | solution.py:226
  232.3 2.3 copy-start.1
  257.5 2.2 copy-start.3
  288.7 9.1 %collective-permute-start.3 = (f32[32,4,1152]{2,1,0:T(4,128)S(1)}, f32[32,4,1152]{2,1,0:T(4,128)S(1)}, u32[]{:S(2)}, u32[]{:S(2)}) collective-permute-start(f32[32,4,1152]{2,1,0:T(4,128)S(1)} %get-tuple-element.11), channel_id=1, source_target_pairs={{1,0},{2,1},{3,2},{4,3},{5,4},{6,5},{7,6},{8,7},{9,8},{10,9},{11,1... | collective-permute-start | bytes 1769480 | tf_op jit(solution)/shard_map/ppermute | solution.py:227
  290.5 12.4 %collective-permute-start.2 = (f32[32,4,1152]{2,1,0:T(4,128)S(1)}, f32[32,4,1152]{2,1,0:T(4,128)S(1)}, u32[]{:S(2)}, u32[]{:S(2)}) collective-permute-start(f32[32,4,1152]{2,1,0:T(4,128)S(1)} %get-tuple-element.12), channel_id=1, source_target_pairs={{0,1},{1,2},{2,3},{3,4},{4,5},{5,6},{6,7},{7,8},{8,9},{9,10},{10,1... | collective-permute-start | bytes 1769480 | tf_op jit(solution)/shard_map/ppermute | solution.py:226
  302.9 2.3 copy-start
  328.1 2.2 copy-start.2
Sparse Core Ops, SparseCore 0:
  8.9 117.1 all-gather.2
  127.6 80.3 all-gather.4

commit v2 on v1

--- a/solution.py
+++ b/solution.py
@@ -152,6 +152,98 @@
     )(field, high, low, gain, keep)
 
 
+def regroup(pieces, lane_group, width, moves):
+    result = None
+    for g, piece in enumerate(pieces):
+        shift = ((g - moves[g]) * width) % LANES
+        piece = pltpu.roll(piece, shift, 1) if shift else piece
+        result = piece if result is None else jnp.where(lane_group == g, piece, result)
+    return result
+
+
+def split_kernel(order, width, field_ref, out_ref):
+    group = LANES // width
+    comps, rows, lons = field_ref.shape
+    lane_group = lax.broadcasted_iota(jnp.int32, (comps, LANES), 1) // width
+    for tile in range(lons // LANES):
+        for band in range(rows // group):
+            pieces = [
+                field_ref[:, band * group + g, tile * LANES : (tile + 1) * LANES] for g in range(group)
+            ]
+            for part in range(group):
+                out_ref[order[tile * group + part], :, band * LANES : (band + 1) * LANES] = regroup(
+                    pieces, lane_group, width, [part] * group
+                )
+
+
+def join_kernel(order, width, blocks_ref, out_ref):
+    group = LANES // width
+    comps, rows, lons = out_ref.shape
+    lane_group = lax.broadcasted_iota(jnp.int32, (comps, LANES), 1) // width
+    for tile in range(lons // LANES):
+        for band in range(rows // group):
+            pieces = [
+                blocks_ref[order[tile * group + part], :, band * LANES : (band + 1) * LANES]
+                for part in range(group)
+            ]
+            for g in range(group):
+                out_ref[:, band * group + g, tile * LANES : (tile + 1) * LANES] = regroup(
+                    pieces, lane_group, width, [g] * group
+                )
+
+
+def tiled(shape, width):
+    local_k, band_rows, lon_count = shape
+    return LANES % width == 0 and band_rows % (LANES // width) == 0 and local_k % 8 == 0
+
+
+def split(field, order, width):
+    local_k, band_rows, lon_count = field.shape
+    count = len(order)
+    if not tiled(field.shape, width):
+        parts = field.reshape(local_k, band_rows, count, width).transpose(2, 0, 1, 3)
+        parts = jnp.stack([parts[order.index(d)] for d in range(count)])
+        return parts.reshape(count, local_k, band_rows * width)
+    return pl.pallas_call(
+        functools.partial(split_kernel, order, width),
+        grid=(local_k // 8,),
+        out_shape=jax.ShapeDtypeStruct((count, local_k, band_rows * width), jnp.float32),
+        in_specs=[pl.BlockSpec((8, band_rows, lon_count), lambda k: (k, 0, 0))],
+        out_specs=pl.BlockSpec((count, 8, band_rows * width), lambda k: (0, k, 0)),
+        name="split",
+    )(field)
+
+
+def join(blocks, order, shape, width):
+    local_k, band_rows, lon_count = shape
+    count = len(order)
+    if not tiled(shape, width):
+        parts = jnp.stack([blocks[d] for d in order]).reshape(count, local_k, band_rows, width)
+        return parts.transpose(1, 2, 0, 3).reshape(shape)
+    return pl.pallas_call(
+        functools.partial(join_kernel, order, width),
+        grid=(local_k // 8,),
+        out_shape=jax.ShapeDtypeStruct(shape, jnp.float32),
+        in_specs=[pl.BlockSpec((count, 8, band_rows * width), lambda k: (0, k, 0))],
+        out_specs=pl.BlockSpec((8, band_rows, lon_count), lambda k: (k, 0, 0)),
+        name="join",
+    )(blocks)
+
+
+def whole_maps(interp_plus, interp_minus, lat_rank, comp_rank, ranks):
+    even = comp_rank % 2 == 0
+    fetched = lax.ppermute(jnp.where(even, interp_plus, interp_minus), "lat", [(0, 1), (1, 0)])
+    shared = lax.ppermute(fetched, "comp", [(i, i ^ 1) for i in range(ranks)])
+    first = lat_rank == 0
+    pieces = []
+    for own, other in (
+        (interp_plus, jnp.where(even, fetched, shared)),
+        (interp_minus, jnp.where(even, shared, fetched)),
+    ):
+        pieces += [jnp.where(first, own, other), jnp.where(first, other, own)]
+    return pieces
+
+
 def body(
     spectrum, interp_plus, interp_minus, source_gain, current, sea_mask, limiter_flags, ice_cells
 ):
@@ -172,14 +264,7 @@
     ]
     block = lat_rank * ranks + jnp.where(lat_rank % 2 == 0, comp_rank, ranks - 1 - comp_rank)
 
-    def snake(blocks):
-        parts = [
-            blocks[band * ranks : (band + 1) * ranks] for band in range(bands)
-        ]
-        return jnp.concatenate([part if band % 2 == 0 else part[::-1] for band, part in enumerate(parts)])
-
-    spread = snake(spectrum.reshape(local_k, band_rows, count, lons).transpose(2, 0, 1, 3))
-    spread = spread.reshape(count, local_k, band_rows * lons)
+    spread = split(spectrum, order, lons)
     gathered = lax.all_to_all(spread, BOTH, split_axis=0, concat_axis=0, tiled=True)
     field = gathered.reshape(bands, comps, band_rows * lons).transpose(0, 2, 1)
     field = field.reshape(rows, lons, comps)
@@ -209,15 +294,10 @@
     iced = jnp.any(cell[:, None] == ice_cells[None, :], axis=1)
     keep = jnp.where(iced, 1.0 - 0.6 * 1.0, 1.0).astype(jnp.float32)[:, None]
 
-    weights = jnp.concatenate(
-        [
-            lax.all_gather(interp_plus, "lat", axis=0, tiled=True),
-            lax.all_gather(interp_minus, "lat", axis=0, tiled=True),
-        ]
-    )
-    rounded = lax.reduce_precision(weights, 8, 7)
-    high = rounded.astype(jnp.bfloat16)
-    low = (weights - rounded).astype(jnp.bfloat16)
+    pieces = whole_maps(interp_plus, interp_minus, lat_rank, comp_rank, ranks)
+    rounded = [lax.reduce_precision(piece, 8, 7) for piece in pieces]
+    high = jnp.concatenate([part.astype(jnp.bfloat16) for part in rounded])
+    low = jnp.concatenate([(piece - part).astype(jnp.bfloat16) for piece, part in zip(pieces, rounded)])
     gain = source_gain[None, :]
 
     eastward = [(order[b], order[(b + 1) % count]) for b in range(count)]
@@ -232,8 +312,7 @@
     spread = field.reshape(bands, band_rows * lons, comps).transpose(0, 2, 1)
     spread = spread.reshape(count, local_k, band_rows * lons)
     gathered = lax.all_to_all(spread, BOTH, split_axis=0, concat_axis=0, tiled=True)
-    blocks = snake(gathered).reshape(count, local_k, band_rows, lons)
-    return blocks.transpose(1, 2, 0, 3).reshape(local_k, band_rows, lon_count)
+    return join(gathered, order, spectrum.shape, lons)
 
 
 def solution(mesh):

time: 518 us -> 428 us (0.83)
  local copies, waits for them, and re-layouts: 100 us -> 27.3 us
  blocking collectives: 172 us -> 127 us
  waiting for transfers between devices: 95.4 us -> 119 us
  Pallas kernels: 100 us -> 119 us
  between operations: 13.6 us -> 0.27 us
    ppermute x0 -> x2, waiting for transfers between devices: none -> 108 us  [the longest x1 108 us: whole_maps(): lax.ppermute(jnp.where(even, interp_plus, interp_minus), 'lat', [(0, 1),...]
    all_gather x2 -> x0, waiting for transfers between devices: 86 us -> none  [the longest x1 76.7 us: body(): lax.all_gather(interp_minus, 'lat', axis=0, tiled=True)]
    all_gather x1, blocking collectives: 57.7 us -> 9.39 us  [body(): statics = lax.all_gather(statics, 'lat', axis=1, tiled=True)]
    pallas_call x0 -> x2, Pallas kernels: none -> 18.7 us  [the longest x1 9.38 us: join(): pl.pallas_call(functools.partial(join_kernel, order, width), grid=(local_...]
    concatenate x3 -> x0, local copies, waits for them, and re-layouts: 17.4 us -> none  [the longest x2 12.2 us: snake(): jnp.concatenate([part if band % 2 == 0 else part[::-1] for band, part in...]
    unnamed x20 -> x26, local copies, waits for them, and re-layouts: 22.1 us -> 6.75 us
    transpose x2 -> x0, local copies, waits for them, and re-layouts: 14.1 us -> none  [the longest x1 8.03 us: body(): return blocks.transpose(1, 2, 0, 3).reshape(local_k, band_rows, lon_count)]
    slice x2 -> x0, local copies, waits for them, and re-layouts: 11.1 us -> none  [snake(): parts = [blocks[band * ranks:(band + 1) * ranks] for band in range(bands)]]
  transfers between devices with their start and end apart: 7 -> 7, of which waited for: 5 -> 5; matrix products, arithmetic and copies ran while one was open for 12% -> 6% of each run, Pallas kernels for 0% -> 0%
where the time goes in v2:
time: 428 us; the launch traced here: 427 us
  blocking collectives  127 us (30%)
  Pallas kernels  119 us (28%)
  waiting for transfers between devices  119 us (28%)
  local copies, waits for them, and re-layouts  27.3 us (6%)
  other arithmetic  20.2 us (5%)
  starting transfers between devices  14.7 us (3%)
    all_to_all x1, blocking collectives, body(): lax.all_to_all(spread, BOTH, split_axis=0, concat_axis=0, tiled=True)  118 us
    ppermute x1, waiting for transfers between devices, whole_maps(): lax.ppermute(jnp.where(even, interp_plus, interp_minus), 'lat', [(0, 1),...  108 us
    pallas_call x2, Pallas kernels, source(): pl.pallas_call(source_kernel, grid=(points // tile,), out_shape=jax.Shape...  54.4 us
    pallas_call x2, Pallas kernels, advect(): pl.pallas_call(advect_kernel, grid=(comps // LANES,), out_shape=jax.Shape...  45.8 us
    all_gather x1, blocking collectives, body(): statics = lax.all_gather(statics, 'lat', axis=1, tiled=True)  9.39 us
    pallas_call x1, Pallas kernels, join(): pl.pallas_call(functools.partial(join_kernel, order, width), grid=(local_...  9.38 us
    pallas_call x1, Pallas kernels, split(): pl.pallas_call(functools.partial(split_kernel, order, width), grid=(local...  9.29 us
    convert_element_type x2, other arithmetic, body(): (piece - part).astype(jnp.bfloat16)  8.58 us
  transfers between devices with their start and end apart: 7, of which 5 were waited for; matrix products, arithmetic and copies ran while one was open for 6% of the time, Pallas kernels for 0%

profile of v2, /device:TPU:0, one launch (start us, length us, event | category | flops | bytes accessed | tf_op | source)
XLA Modules:
  0.0 427.5 jit_solution(1318694830228876503)
XLA Ops:
  0.0 9.3 %split.1 = f32[32,72,512]{2,1,0:T(8,128)} custom-call(f32[72,16,1024]{2,1,0:T(8,128)} %field_ref.1), custom_call_target="tpu_custom_call" | custom-call | tf_op jit(solution)/shard_map/split/pallas_call | solution.py:207
  9.3 7.4 %all-to-all-start = ((f32[32,72,512]{2,1,0:T(8,128)}), f32[32,72,512]{2,1,0:T(8,128)}, u32[]{:S(2)}, u32[]{:S(2)}) async-start(f32[32,72,512]{2,1,0:T(8,128)} %split.1), calls=%async_computation | async-start | bytes 9437184 | tf_op jit(solution)/shard_map/all_to_all | solution.py:268
  16.7 0.0 copy-done.3
  16.7 0.0 copy-start.7
  16.7 0.0 copy-start.8
  16.8 0.0 copy-start.6
  16.8 0.0 copy-start.9
  16.8 0.0 copy-start.10
  16.8 0.3 broadcast_select_fusion.2
  17.1 1.8 collective-permute-start.2
  18.9 108.2 %collective-permute-done.2 = f32[576,1152]{1,0:T(8,128)} collective-permute-done((f32[576,1152]{1,0:T(8,128)S(1)}, f32[576,1152]{1,0:T(8,128)}, u32[]{:S(2)}, u32[]{:S(2)}) %collective-permute-start.2) | collective-permute-done | bytes 2654240 | tf_op jit(solution)/shard_map/ppermute | solution.py:235
  127.0 0.0 collective-permute-start.3
  127.0 0.0 copy-done.7
  127.0 0.0 copy-done.8
  127.0 0.0 copy-done.6
  127.1 9.4 %all_gather.3 = f32[4,32,1024]{2,1,0:T(8,128)S(1)} all-gather(f32[4,16,1024]{2,1,0:T(8,128)S(1)} %pad_maximum_fusion.2), channel_id=1, replica_groups=mesh['lat'=2,'comp'=16] {'lat'}, dimensions={1}, use_global_device_ids=true | all-gather | bytes 786432 | tf_op jit(solution)/shard_map/all_gather | solution.py:275
  136.5 0.1 slice.55
  136.6 0.0 copy-done.9
  136.6 0.6 broadcast_in_dim.20.gain_ref
  137.2 0.1 iota_add_fusion
  137.3 0.1 add.143
  137.3 0.0 copy-done.10
  137.3 0.7 compare_reduce_fusion
  138.0 1.0 copy.16.keep_ref
  139.0 1.1 concatenate.9
  140.1 0.9 dynamic-slice_bitcast_fusion
  141.0 0.2 sine_multiply_fusion
  141.2 0.1 fusion.6
  141.3 0.0 collective-permute-done.3
  141.3 4.5 %fusion = (bf16[576,1152]{1,0:T(8,128)(2,1)S(1)}, f32[576,1152]{1,0:T(8,128)S(1)}, bf16[576,1152]{1,0:T(8,128)(2,1)S(1)}, f32[576,1152]{1,0:T(8,128)S(1)}) fusion(f32[576,1152]{1,0:T(8,128)S(1)} %copy-done.3, pred[]{:T(512)S(6)} %eq.28, f32[576,1152]{1,0:T(8,128)} %collective-permute-done.2, f32[576,1152]{1,0:T(8,128)} %collective-permute-done.3, ...), kind=kLoop, calls=%fused_computation.11 | loop fusion | flops 6635520 | bytes 18579458 | tf_op jit(solution)/shard_map/convert_element_type | solution.py:300
  145.8 0.0 copy-done.4
  145.8 4.1 fusion.1
  149.9 4.0 pad_maximum_fusion.1.low_ref
  153.9 0.0 all-to-all-done
  153.9 6.0 %copy.15 = f32[2,1152,512]{1,2,0:T(8,128)} copy(f32[2,1152,512]{2,1,0:T(8,128)} %bitcast.6) | data formatting | bytes 9437184 | tf_op jit(solution)/shard_map/reshape | solution.py:269
  159.9 1.9 fusion.15
  161.9 0.1 collective-permute-start.1
  161.9 0.5 collective-permute-start
  162.4 6.3 %pad_maximum_fusion.high_ref = bf16[2304,1152]{1,0:T(8,128)(2,1)} fusion(bf16[576,1152]{1,0:T(8,128)(2,1)} %get-tuple-element.30, bf16[576,1152]{1,0:T(8,128)(2,1)} %get-tuple-element.29, bf16[576,1152]{1,0:T(8,128)(2,1)S(1)} %copy-done.5, bf16[576,1152]{1,0:T(8,128)(2,1)} %get-tuple-element.11), kind=kLoop, calls=%fused_computation | loop fusion | flops 21233664 | bytes 10616832 | tf_op jit(solution)/shard_map/concatenate | solution.py:299
  168.7 0.6 collective-permute-done.1.right_ref
  169.3 2.7 collective-permute-done.left_ref
  172.1 0.2 broadcast_in_dim.16.uf_ref
  172.3 0.2 broadcast_in_dim.19.sea_ref
  172.5 0.2 broadcast_in_dim.17.vf_ref
  172.8 0.2 broadcast_in_dim.18.flag_ref
  173.0 0.0 slice-done
  173.0 0.0 slice-done.1
  173.0 22.9 %advect.2 = f32[32,32,1152]{2,1,0:T(8,128)S(1)} custom-call(f32[1,1152]{1,0:T(1,128)S(1)} %get-tuple-element.28.cx_ref, f32[1,1152]{1,0:T(1,128)S(1)} %get-tuple-element.27.cy_ref, f32[32,40,128]{2,1,0:T(8,128)S(1)} %broadcast_in_dim.16.uf_ref, f32[33,40,128]{2,1,0:T(8,128)S(1)} %broadcast_in_dim.17.vf_ref, f32[33,40,128]{2,1,0:T(8,128)S(1)} %broadcast_in_dim.18.flag_ref, ...), custom_call_target="tpu_custom_call" | custom-call | tf_op jit(solution)/shard_map/advect/pallas_call | solution.py:92
  195.9 0.0 copy-start.2
  195.9 2.2 copy-done.2
  198.1 27.2 %source.2 = f32[1024,1152]{1,0:T(8,128)} custom-call(f32[1024,1152]{1,0:T(8,128)} %bitcast.34, bf16[2304,1152]{1,0:T(8,128)(2,1)} %pad_maximum_fusion.high_ref, bf16[2304,1152]{1,0:T(8,128)(2,1)} %pad_maximum_fusion.1.low_ref, f32[1,1152]{1,0:T(1,128)} %broadcast_in_dim.20.gain_ref, f32[1024,1]{1,0:T(8,128)} %copy.16.keep_ref), custom_call_target="tpu_custom_call" | custom-call | tf_op jit(solution)/shard_map/source/pallas_call | solution.py:138
  225.3 1.8 fusion.14
  227.1 0.1 collective-permute-start.5
  227.2 4.9 %collective-permute-start.4 = (f32[32,4,1152]{2,1,0:T(4,128)S(1)}, f32[32,4,1152]{2,1,0:T(4,128)S(1)}, u32[]{:S(2)}, u32[]{:S(2)}) collective-permute-start(f32[32,4,1152]{2,1,0:T(4,128)S(1)} %get-tuple-element.18), channel_id=1, source_target_pairs={{0,1},{1,2},{2,3},{3,4},{4,5},{5,6},{6,7},{7,8},{8,9},{9,10},{10,1... | collective-permute-start | bytes 1769480 | tf_op jit(solution)/shard_map/ppermute | solution.py:306
  232.1 2.5 collective-permute-done.5.right_ref
  234.6 4.8 %collective-permute-done.4.left_ref = f32[32,4,1152]{2,1,0:T(4,128)S(1)} collective-permute-done((f32[32,4,1152]{2,1,0:T(4,128)S(1)}, f32[32,4,1152]{2,1,0:T(4,128)S(1)}, u32[]{:S(2)}, u32[]{:S(2)}) %collective-permute-start.4) | collective-permute-done | bytes 589856 | tf_op jit(solution)/shard_map/ppermute | solution.py:306
  239.4 2.3 copy-done
  241.8 22.9 %advect.3 = f32[32,32,1152]{2,1,0:T(8,128)S(1)} custom-call(f32[1,1152]{1,0:T(1,128)S(1)} %get-tuple-element.28.cx_ref, f32[1,1152]{1,0:T(1,128)S(1)} %get-tuple-element.27.cy_ref, f32[32,40,128]{2,1,0:T(8,128)S(1)} %broadcast_in_dim.16.uf_ref, f32[33,40,128]{2,1,0:T(8,128)S(1)} %broadcast_in_dim.17.vf_ref, f32[33,40,128]{2,1,0:T(8,128)S(1)} %broadcast_in_dim.18.flag_ref, ...), custom_call_target="tpu_custom_call" | custom-call | tf_op jit(solution)/shard_map/advect/pallas_call | solution.py:92
  264.7 0.0 copy-start.1
  264.7 2.2 copy-done.1
  266.8 27.2 %source.3 = f32[1024,1152]{1,0:T(8,128)} custom-call(f32[1024,1152]{1,0:T(8,128)} %bitcast.33, bf16[2304,1152]{1,0:T(8,128)(2,1)} %pad_maximum_fusion.high_ref, bf16[2304,1152]{1,0:T(8,128)(2,1)} %pad_maximum_fusion.1.low_ref, f32[1,1152]{1,0:T(1,128)} %broadcast_in_dim.20.gain_ref, f32[1024,1]{1,0:T(8,128)} %copy.16.keep_ref), custom_call_target="tpu_custom_call" | custom-call | tf_op jit(solution)/shard_map/source/pallas_call | solution.py:138
  294.0 6.0 %copy.18 = f32[2,512,1152]{1,2,0:T(8,128)} copy(f32[2,512,1152]{2,1,0:T(8,128)} %bitcast.35) | data formatting | bytes 9437184 | tf_op jit(solution)/shard_map/reshape;reshape | solution.py:312
  300.1 118.0 %all_to_all.10.blocks_ref = f32[32,72,512]{2,1,0:T(8,128)} all-to-all(f32[32,72,512]{2,1,0:T(8,128)} %bitcast.36), channel_id=1, replica_groups=mesh['lat'=2,'comp'=16] {'lat','comp'}, dimensions={0} | all-to-all | bytes 9437184 | tf_op jit(solution)/shard_map/all_to_all | solution.py:314
  418.1 9.4 %join.1 = f32[72,16,1024]{2,1,0:T(8,128)} custom-call(f32[32,72,512]{2,1,0:T(8,128)} %all_to_all.10.blocks_ref), custom_call_target="tpu_custom_call" | custom-call | tf_op jit(solution)/shard_map/join/pallas_call | solution.py:223
  (15 shorter events, 0.1 us)
Async XLA Ops:
  9.3 7.4 %copy-start.3 = (f32[576,1152]{1,0:T(8,128)S(1)}, f32[576,1152]{1,0:T(8,128)}, u32[]{:S(2)}) copy-start(f32[576,1152]{1,0:T(8,128)} %param.9) | copy-start | bytes 7962628
  9.3 144.6 %all-to-all-start = ((f32[32,72,512]{2,1,0:T(8,128)}), f32[32,72,512]{2,1,0:T(8,128)}, u32[]{:S(2)}, u32[]{:S(2)}) async-start(f32[32,72,512]{2,1,0:T(8,128)} %split.1), calls=%async_computation | async-start | bytes 9437184 | tf_op jit(solution)/shard_map/all_to_all | solution.py:268
  16.7 110.3 %copy-start.7 = (s32[16,1024]{1,0:T(8,128)S(1)}, s32[16,1024]{1,0:T(8,128)}, u32[]{:S(2)}) copy-start(s32[16,1024]{1,0:T(8,128)} %param.13) | copy-start | bytes 196612
  16.7 110.3 %copy-start.8 = (s32[16,1024]{1,0:T(8,128)S(1)}, s32[16,1024]{1,0:T(8,128)}, u32[]{:S(2)}) copy-start(s32[16,1024]{1,0:T(8,128)} %param.14) | copy-start | bytes 196612
  16.8 110.3 %copy-start.6 = (f32[2,16,1024]{2,1,0:T(8,128)S(1)}, f32[2,16,1024]{2,1,0:T(8,128)}, u32[]{:S(2)}) copy-start(f32[2,16,1024]{2,1,0:T(8,128)} %param.12) | copy-start | bytes 393220
  16.8 119.8 %copy-start.9 = (f32[1152]{0:T(1024)S(1)}, f32[1152]{0:T(1024)}, u32[]{:S(2)}) copy-start(f32[1152]{0:T(1024)} %param.11) | copy-start | bytes 13828
  16.8 120.5 %copy-start.10 = (s32[1024]{0:T(1024)S(1)}, s32[1024]{0:T(1024)}, u32[]{:S(2)}) copy-start(s32[1024]{0:T(1024)} %param.15) | copy-start | bytes 12292
  17.1 109.9 %collective-permute-start.2 = (f32[576,1152]{1,0:T(8,128)S(1)}, f32[576,1152]{1,0:T(8,128)}, u32[]{:S(2)}, u32[]{:S(2)}) collective-permute-start(f32[576,1152]{1,0:T(8,128)S(1)} %broadcast_select_fusion.2), channel_id=1, source_target_pairs={{0,16},{16,0},{1,17},{17,1},{2,18},{18,2},{3,19},{19,3},{4,20},{20... | collective-permute-start | bytes 7962632 | tf_op jit(solution)/shard_map/ppermute | solution.py:235
  127.0 14.2 %collective-permute-start.3 = (f32[576,1152]{1,0:T(8,128)}, f32[576,1152]{1,0:T(8,128)}, u32[]{:S(2)}, u32[]{:S(2)}) collective-permute-start(f32[576,1152]{1,0:T(8,128)} %collective-permute-done.2), channel_id=1, source_target_pairs={{0,1},{1,0},{2,3},{3,2},{4,5},{5,4},{6,7},{7,6},{8,9},{9,8},{10,11... | collective-permute-start | bytes 7962632 | tf_op jit(solution)/shard_map/ppermute | solution.py:236
  141.3 4.5 %copy-start.4 = (f32[576,1152]{1,0:T(8,128)S(1)}, f32[576,1152]{1,0:T(8,128)}, u32[]{:S(2)}) copy-start(f32[576,1152]{1,0:T(8,128)} %param.10) | copy-start | bytes 7962628
  159.9 2.5 copy-start.5
  161.9 7.5 %collective-permute-start.1 = (f32[32,4,1152]{2,1,0:T(4,128)S(1)}, f32[32,4,1152]{2,1,0:T(4,128)S(1)}, u32[]{:S(2)}, u32[]{:S(2)}) collective-permute-start(f32[32,4,1152]{2,1,0:T(4,128)S(1)} %get-tuple-element.19), channel_id=1, source_target_pairs={{1,0},{2,1},{3,2},{4,3},{5,4},{6,5},{7,6},{8,7},{9,8},{10,9},{11,1... | collective-permute-start | bytes 1769480 | tf_op jit(solution)/shard_map/ppermute | solution.py:307
  161.9 10.1 %collective-permute-start = (f32[32,4,1152]{2,1,0:T(4,128)S(1)}, f32[32,4,1152]{2,1,0:T(4,128)S(1)}, u32[]{:S(2)}, u32[]{:S(2)}) collective-permute-start(f32[32,4,1152]{2,1,0:T(4,128)S(1)} %get-tuple-element.20), channel_id=1, source_target_pairs={{0,1},{1,2},{2,3},{3,4},{4,5},{5,6},{6,7},{7,8},{8,9},{9,10},{10,1... | collective-permute-start | bytes 1769480 | tf_op jit(solution)/shard_map/ppermute | solution.py:306
  162.4 10.6 %slice-start = ((s8[4718592]{0:T(1024)(128)(4,1)}), s8[4194304]{0:T(1024)(128)(4,1)S(1)}, s32[]{:S(2)}) async-start(s8[4718592]{0:T(1024)(128)(4,1)} %bitcast.30), calls=%async_computation.2 | async-start | bytes 8388608
  162.4 10.6 %slice-start.1 = ((s8[4718592]{0:T(1024)(128)(4,1)}), s8[524288]{0:T(1024)(128)(4,1)S(1)}, s32[]{:S(2)}) async-start(s8[4718592]{0:T(1024)(128)(4,1)} %bitcast.30), calls=%async_computation.3 | async-start | bytes 1048576
  195.9 2.2 copy-start.2
  227.1 7.5 %collective-permute-start.5 = (f32[32,4,1152]{2,1,0:T(4,128)S(1)}, f32[32,4,1152]{2,1,0:T(4,128)S(1)}, u32[]{:S(2)}, u32[]{:S(2)}) collective-permute-start(f32[32,4,1152]{2,1,0:T(4,128)S(1)} %get-tuple-element.17), channel_id=1, source_target_pairs={{1,0},{2,1},{3,2},{4,3},{5,4},{6,5},{7,6},{8,7},{9,8},{10,9},{11,1... | collective-permute-start | bytes 1769480 | tf_op jit(solution)/shard_map/ppermute | solution.py:307
  227.2 12.2 %collective-permute-start.4 = (f32[32,4,1152]{2,1,0:T(4,128)S(1)}, f32[32,4,1152]{2,1,0:T(4,128)S(1)}, u32[]{:S(2)}, u32[]{:S(2)}) collective-permute-start(f32[32,4,1152]{2,1,0:T(4,128)S(1)} %get-tuple-element.18), channel_id=1, source_target_pairs={{0,1},{1,2},{2,3},{3,4},{4,5},{5,6},{6,7},{7,8},{8,9},{9,10},{10,1... | collective-permute-start | bytes 1769480 | tf_op jit(solution)/shard_map/ppermute | solution.py:306
  239.4 2.3 copy-start
  264.7 2.2 copy-start.1

commit v3 on v2

--- a/solution.py
+++ b/solution.py
@@ -111,7 +111,7 @@
     )(speed_x, speed_y, face_u, face_v, flag, sea, field, left, right)
 
 
-def source_kernel(field_ref, high_ref, low_ref, gain_ref, keep_ref, out_ref):
+def source_kernel(turned, field_ref, high_ref, low_ref, gain_ref, keep_ref, out_ref):
     comps = field_ref.shape[1]
     field = field_ref[...]
     field_high = field.astype(jnp.bfloat16)
@@ -129,25 +129,44 @@
     gain = gain_ref[...]
     forcing = field * (field * (plus + minus) - 2.0 * plus * minus)
     update = gain * forcing / (1.0 + gain * (plus * plus + minus * minus))
-    out_ref[...] = (field + update) * keep_ref[...]
-
-
-def source(field, high, low, gain, keep):
+    result = (field + update) * keep_ref[...]
+    if turned:
+        out_ref[0] = result.T
+    else:
+        out_ref[...] = result
+
+
+def source(field, high, low, gain, keep, bands=0, half=0):
     points, comps = field.shape
-    tile = min(256, points)
+    if bands:
+        tile = points // (2 * bands)
+        grid = (bands,)
+        place = lambda p: (2 * p + half, 0)
+        result = jax.ShapeDtypeStruct((bands, comps, tile), jnp.float32)
+        out_spec = pl.BlockSpec((1, comps, tile), lambda p: (p, 0, 0))
+    else:
+        tile = min(256, points)
+        grid = (points // tile,)
+        place = lambda p: (p, 0)
+        result = jax.ShapeDtypeStruct(field.shape, jnp.float32)
+        out_spec = pl.BlockSpec((tile, comps), place)
+    work = grid[0] * tile * comps
     return pl.pallas_call(
-        source_kernel,
-        grid=(points // tile,),
-        out_shape=jax.ShapeDtypeStruct(field.shape, jnp.float32),
+        functools.partial(source_kernel, bands > 0),
+        grid=grid,
+        out_shape=result,
         in_specs=[
-            pl.BlockSpec((tile, comps), lambda p: (p, 0)),
+            pl.BlockSpec((tile, comps), place),
             pl.BlockSpec(high.shape, lambda p: (0, 0)),
             pl.BlockSpec(low.shape, lambda p: (0, 0)),
             pl.BlockSpec((1, comps), lambda p: (0, 0)),
-            pl.BlockSpec((tile, 1), lambda p: (p, 0)),
+            pl.BlockSpec((tile, 1), place),
         ],
-        out_specs=pl.BlockSpec((tile, comps), lambda p: (p, 0)),
+        out_specs=out_spec,
         compiler_params=pltpu.CompilerParams(vmem_limit_bytes=56 * 2**20),
+        cost_estimate=pl.CostEstimate(
+            flops=12 * work * comps, bytes_accessed=8 * work + 8 * comps * comps, transcendentals=0
+        ),
         name="source",
     )(field, high, low, gain, keep)
 
@@ -176,14 +195,17 @@
                 )
 
 
-def join_kernel(order, width, blocks_ref, out_ref):
+def join_kernel(order, width, upper_ref, lower_ref, out_ref):
     group = LANES // width
     comps, rows, lons = out_ref.shape
     lane_group = lax.broadcasted_iota(jnp.int32, (comps, LANES), 1) // width
     for tile in range(lons // LANES):
         for band in range(rows // group):
+            middle = rows // group // 2
+            half_ref = upper_ref if band < middle else lower_ref
+            start = (band % middle) * LANES
             pieces = [
-                blocks_ref[order[tile * group + part], :, band * LANES : (band + 1) * LANES]
+                half_ref[order[tile * group + part], :, start : start + LANES]
                 for part in range(group)
             ]
             for g in range(group):
@@ -194,7 +216,7 @@
 
 def tiled(shape, width):
     local_k, band_rows, lon_count = shape
-    return LANES % width == 0 and band_rows % (LANES // width) == 0 and local_k % 8 == 0
+    return LANES % width == 0 and band_rows % (2 * LANES // width) == 0 and local_k % 8 == 0
 
 
 def split(field, order, width):
@@ -214,34 +236,65 @@
     )(field)
 
 
-def join(blocks, order, shape, width):
+def join(upper, lower, order, shape, width):
     local_k, band_rows, lon_count = shape
     count = len(order)
     if not tiled(shape, width):
+        blocks = jnp.concatenate([upper, lower], axis=2)
         parts = jnp.stack([blocks[d] for d in order]).reshape(count, local_k, band_rows, width)
         return parts.transpose(1, 2, 0, 3).reshape(shape)
     return pl.pallas_call(
         functools.partial(join_kernel, order, width),
         grid=(local_k // 8,),
         out_shape=jax.ShapeDtypeStruct(shape, jnp.float32),
-        in_specs=[pl.BlockSpec((count, 8, band_rows * width), lambda k: (0, k, 0))],
+        in_specs=[pl.BlockSpec((count, 8, band_rows * width // 2), lambda k: (0, k, 0))] * 2,
         out_specs=pl.BlockSpec((8, band_rows, lon_count), lambda k: (k, 0, 0)),
         name="join",
-    )(blocks)
-
-
-def whole_maps(interp_plus, interp_minus, lat_rank, comp_rank, ranks):
-    even = comp_rank % 2 == 0
-    fetched = lax.ppermute(jnp.where(even, interp_plus, interp_minus), "lat", [(0, 1), (1, 0)])
+    )(upper, lower)
+
+
+def maps_kernel(rank_ref, plus_ref, minus_ref, fetched_ref, shared_ref, high_ref, low_ref):
+    lat_rank = rank_ref[0]
+    even = rank_ref[1] == 0
+
+    def put(quarter, piece_ref):
+        piece = piece_ref[...]
+        rounded = piece.astype(jnp.bfloat16)
+        high_ref[quarter] = rounded
+        low_ref[quarter] = (piece - rounded.astype(jnp.float32)).astype(jnp.bfloat16)
+
+    put(lat_rank, plus_ref)
+    put(2 + lat_rank, minus_ref)
+
+    @pl.when(even)
+    def _():
+        put(1 - lat_rank, fetched_ref)
+        put(3 - lat_rank, shared_ref)
+
+    @pl.when(jnp.logical_not(even))
+    def _():
+        put(1 - lat_rank, shared_ref)
+        put(3 - lat_rank, fetched_ref)
+
+
+def whole_maps(interp_plus, interp_minus, fetched, lat_rank, comp_rank, ranks):
     shared = lax.ppermute(fetched, "comp", [(i, i ^ 1) for i in range(ranks)])
-    first = lat_rank == 0
-    pieces = []
-    for own, other in (
-        (interp_plus, jnp.where(even, fetched, shared)),
-        (interp_minus, jnp.where(even, shared, fetched)),
-    ):
-        pieces += [jnp.where(first, own, other), jnp.where(first, other, own)]
-    return pieces
+    rows, comps = interp_plus.shape
+    tile = rows // 6
+    result = jax.ShapeDtypeStruct((4, rows, comps), jnp.bfloat16)
+    high, low = pl.pallas_call(
+        maps_kernel,
+        grid_spec=pltpu.PrefetchScalarGridSpec(
+            num_scalar_prefetch=1,
+            grid=(rows // tile,),
+            in_specs=[pl.BlockSpec((tile, comps), lambda p, rank: (p, 0))] * 4,
+            out_specs=[pl.BlockSpec((4, tile, comps), lambda p, rank: (0, p, 0))] * 2,
+        ),
+        out_shape=[result, result],
+        compiler_params=pltpu.CompilerParams(vmem_limit_bytes=24 * 2**20),
+        name="maps",
+    )(jnp.stack([lat_rank, comp_rank % 2]), interp_plus, interp_minus, fetched, shared)
+    return high.reshape(4 * rows, comps), low.reshape(4 * rows, comps)
 
 
 def body(
@@ -264,6 +317,9 @@
     ]
     block = lat_rank * ranks + jnp.where(lat_rank % 2 == 0, comp_rank, ranks - 1 - comp_rank)
 
+    send = jnp.where(comp_rank % 2 == 0, interp_plus, interp_minus)
+    spectrum, send = lax.optimization_barrier((spectrum, send))
+    fetched = lax.ppermute(send, "lat", [(0, 1), (1, 0)])
     spread = split(spectrum, order, lons)
     gathered = lax.all_to_all(spread, BOTH, split_axis=0, concat_axis=0, tiled=True)
     field = gathered.reshape(bands, comps, band_rows * lons).transpose(0, 2, 1)
@@ -294,10 +350,7 @@
     iced = jnp.any(cell[:, None] == ice_cells[None, :], axis=1)
     keep = jnp.where(iced, 1.0 - 0.6 * 1.0, 1.0).astype(jnp.float32)[:, None]
 
-    pieces = whole_maps(interp_plus, interp_minus, lat_rank, comp_rank, ranks)
-    rounded = [lax.reduce_precision(piece, 8, 7) for piece in pieces]
-    high = jnp.concatenate([part.astype(jnp.bfloat16) for part in rounded])
-    low = jnp.concatenate([(piece - part).astype(jnp.bfloat16) for piece, part in zip(pieces, rounded)])
+    high, low = whole_maps(interp_plus, interp_minus, fetched, lat_rank, comp_rank, ranks)
     gain = source_gain[None, :]
 
     eastward = [(order[b], order[(b + 1) % count]) for b in range(count)]
@@ -306,13 +359,16 @@
         left = lax.ppermute(field[:, lons - HALO :], BOTH, eastward)
         right = lax.ppermute(field[:, :HALO], BOTH, westward)
         field = advect(field, left, right, fixed)
-        field = source(field.reshape(rows * lons, comps), high, low, gain, keep)
-        field = field.reshape(rows, lons, comps)
-
-    spread = field.reshape(bands, band_rows * lons, comps).transpose(0, 2, 1)
-    spread = spread.reshape(count, local_k, band_rows * lons)
-    gathered = lax.all_to_all(spread, BOTH, split_axis=0, concat_axis=0, tiled=True)
-    return join(gathered, order, spectrum.shape, lons)
+        field = field.reshape(rows * lons, comps)
+        if outer_step < OUTER - 1:
+            field = source(field, high, low, gain, keep).reshape(rows, lons, comps)
+
+    halves = []
+    for half in range(2):
+        spread = source(field, high, low, gain, keep, bands, half)
+        spread = spread.reshape(count, local_k, band_rows * lons // 2)
+        halves.append(lax.all_to_all(spread, BOTH, split_axis=0, concat_axis=0, tiled=True))
+    return join(halves[0], halves[1], order, spectrum.shape, lons)
 
 
 def solution(mesh):

time: 428 us -> 410 us (0.958)
  blocking collectives: 127 us -> 68.3 us
  waiting for transfers between devices: 119 us -> 157 us
  other arithmetic: 20.2 us -> 3.13 us
  Pallas kernels: 119 us -> 131 us
  starting transfers between devices: 14.7 us -> 21.3 us
    all_to_all x1, blocking collectives: 118 us -> 58.9 us  [body(): lax.all_to_all(spread, BOTH, split_axis=0, concat_axis=0, tiled=True)]
    all_to_all x1 -> x2, waiting for transfers between devices: 0.01 us -> 38.8 us  [body(): lax.all_to_all(spread, BOTH, split_axis=0, concat_axis=0, tiled=True)]
    pallas_call x2 -> x4, Pallas kernels: 54.4 us -> 66.2 us  [the longest x3 60.3 us: source(): pl.pallas_call(functools.partial(source_kernel, bands > 0), grid=grid, ou...]
    concatenate x2 -> x0, other arithmetic: 10.3 us -> none  [the longest x1 6.3 us: body(): high = jnp.concatenate([part.astype(jnp.bfloat16) for part in rounded])]
    all_to_all x1 -> x2, starting transfers between devices: 7.41 us -> 17.1 us  [body(): lax.all_to_all(spread, BOTH, split_axis=0, concat_axis=0, tiled=True)]
    convert_element_type x2 -> x0, other arithmetic: 8.58 us -> none  [body(): (piece - part).astype(jnp.bfloat16)]
    unnamed x26 -> x30, local copies, waits for them, and re-layouts: 6.75 us -> 13.4 us
    another operation x1 -> x0, local copies, waits for them, and re-layouts: 6.04 us -> none  [body(): spread = field.reshape(bands, band_rows * lons, comps).transpose(0, 2, 1)]
  transfers between devices with their start and end apart: 7 -> 8, of which waited for: 5 -> 4; matrix products, arithmetic and copies ran while one was open for 6% -> 3% of each run, Pallas kernels for 0% -> 6%
where the time goes in v3:
time: 410 us; the launch traced here: 409 us
  waiting for transfers between devices  157 us (38%)
  Pallas kernels  131 us (32%)
  blocking collectives  68.3 us (17%)
  local copies, waits for them, and re-layouts  27.4 us (7%)
  starting transfers between devices  21.3 us (5%)
    ppermute x1, waiting for transfers between devices, body(): fetched = lax.ppermute(send, 'lat', [(0, 1), (1, 0)])  109 us
    pallas_call x3, Pallas kernels, source(): pl.pallas_call(functools.partial(source_kernel, bands > 0), grid=grid, ou...  60.3 us
    all_to_all x1, blocking collectives, body(): lax.all_to_all(spread, BOTH, split_axis=0, concat_axis=0, tiled=True)  58.9 us
    pallas_call x2, Pallas kernels, advect(): pl.pallas_call(advect_kernel, grid=(comps // LANES,), out_shape=jax.Shape...  46.5 us
    all_to_all x2, waiting for transfers between devices, body(): lax.all_to_all(spread, BOTH, split_axis=0, concat_axis=0, tiled=True)  38.8 us
    all_to_all x2, starting transfers between devices, body(): lax.all_to_all(spread, BOTH, split_axis=0, concat_axis=0, tiled=True)  17.1 us
    unnamed x30, local copies, waits for them, and re-layouts  13.4 us
    all_gather x1, blocking collectives, body(): statics = lax.all_gather(statics, 'lat', axis=1, tiled=True)  9.39 us
  transfers between devices with their start and end apart: 8, of which 4 were waited for; matrix products, arithmetic and copies ran while one was open for 3% of the time, Pallas kernels for 6%

profile of v3, /device:TPU:0, one launch (start us, length us, event | category | flops | bytes accessed | tf_op | source)
XLA Modules:
  0.0 409.0 jit_solution(14220240031077141914)
XLA Ops:
  0.0 2.0 broadcast_select_fusion
  2.0 9.3 %split.1 = f32[32,72,512]{2,1,0:T(8,128)} custom-call(f32[72,16,1024]{2,1,0:T(8,128)} %field_ref), custom_call_target="tpu_custom_call" | custom-call | tf_op jit(solution)/shard_map/split/pallas_call | solution.py:229
  11.3 7.4 %all-to-all-start = ((f32[32,72,512]{2,1,0:T(8,128)}), f32[32,72,512]{2,1,0:T(8,128)}, u32[]{:S(2)}, u32[]{:S(2)}) async-start(f32[32,72,512]{2,1,0:T(8,128)} %split.1), calls=%async_computation | async-start | bytes 9437184 | tf_op jit(solution)/shard_map/all_to_all | solution.py:324
  18.8 1.8 collective-permute-start.2
  20.5 108.5 %collective-permute-done.2.fetched_ref = f32[576,1152]{1,0:T(8,128)} collective-permute-done((f32[576,1152]{1,0:T(8,128)S(1)}, f32[576,1152]{1,0:T(8,128)}, u32[]{:S(2)}, u32[]{:S(2)}) %collective-permute-start.2) | collective-permute-done | bytes 2654240 | tf_op jit(solution)/shard_map/ppermute | solution.py:322
  129.1 0.0 collective-permute-start.3
  129.1 0.0 copy-done.9
  129.1 0.0 copy-done.10
  129.1 0.0 copy-done.8
  129.1 9.4 %all_gather.3 = f32[4,32,1024]{2,1,0:T(8,128)S(1)} all-gather(f32[4,16,1024]{2,1,0:T(8,128)S(1)} %pad_maximum_fusion), channel_id=1, replica_groups=mesh['lat'=2,'comp'=16] {'lat'}, dimensions={1}, use_global_device_ids=true | all-gather | bytes 786432 | tf_op jit(solution)/shard_map/all_gather | solution.py:331
  138.5 0.1 slice.55
  138.6 0.1 iota_add_fusion
  138.7 0.1 add.144
  138.8 0.3 concatenate.3
  139.1 0.1 dynamic-slice_bitcast_fusion
  139.2 0.0 copy-done.12
  139.2 0.7 compare_reduce_fusion
  139.9 0.0 all-to-all-done
  139.9 0.0 copy-start.11
  139.9 0.0 copy-start
  139.9 6.2 %copy.14 = f32[2,1152,512]{1,2,0:T(8,128)} copy(f32[2,1152,512]{2,1,0:T(8,128)} %bitcast.6) | data formatting | bytes 9437184 | tf_op jit(solution)/shard_map/reshape | solution.py:325
  146.2 2.9 fusion.11
  149.0 0.4 collective-permute-start.1
  149.4 0.2 collective-permute-start
  149.5 0.1 pad_add_fusion.rank_ref
  149.6 0.0 copy-done.11
  149.6 0.6 broadcast_in_dim.20.gain_ref
  150.2 1.0 copy.15.keep_ref
  151.2 0.2 sine_multiply_fusion
  151.4 0.0 slice-start
  151.4 0.1 fusion.2
  151.5 0.0 collective-permute-done.3.shared_ref
  151.5 0.0 copy-done
  151.5 0.0 copy-start.1
  151.5 1.9 copy-done.1
  153.4 6.0 %maps.1 = (bf16[4,576,1152]{2,1,0:T(8,128)(2,1)S(1)}, bf16[4,576,1152]{2,1,0:T(8,128)(2,1)S(1)}) custom-call(s32[2]{0:T(128)S(1)} %pad_add_fusion.rank_ref, f32[576,1152]{1,0:T(8,128)S(1)} %copy-done, f32[576,1152]{1,0:T(8,128)S(1)} %copy-done.1, f32[576,1152]{1,0:T(8,128)} %collective-permute-done.2.fetched_ref, f32[576,1152]{1,0:T(8,128)} %collective-permute-done.3.shared_ref), custom_call_target="tpu_custom_call" | custom-call | tf_op jit(solution)/shard_map/maps/pallas_call | solution.py:285
  159.4 0.0 copy-start.5
  159.4 2.4 copy-done.5
  161.8 2.4 copy-done.6
  164.2 0.0 collective-permute-done.1.right_ref
  164.2 0.0 collective-permute-done.left_ref
  164.2 0.2 broadcast_in_dim.16.uf_ref
  164.4 0.2 broadcast_in_dim.19.sea_ref
  164.6 0.2 broadcast_in_dim.17.vf_ref
  164.9 0.2 broadcast_in_dim.18.flag_ref
  165.2 23.6 %advect.2 = f32[32,32,1152]{2,1,0:T(8,128)S(1)} custom-call(f32[1,1152]{1,0:T(1,128)S(1)} %get-tuple-element.24.cx_ref, f32[1,1152]{1,0:T(1,128)S(1)} %get-tuple-element.23.cy_ref, f32[32,40,128]{2,1,0:T(8,128)S(1)} %broadcast_in_dim.16.uf_ref, f32[33,40,128]{2,1,0:T(8,128)S(1)} %broadcast_in_dim.17.vf_ref, f32[33,40,128]{2,1,0:T(8,128)S(1)} %broadcast_in_dim.18.flag_ref, ...), custom_call_target="tpu_custom_call" | custom-call | tf_op jit(solution)/shard_map/advect/pallas_call | solution.py:92
  188.8 0.0 copy-start.4
  188.8 2.2 copy-done.4
  191.0 27.2 %source.3 = f32[1024,1152]{1,0:T(8,128)} custom-call(f32[1024,1152]{1,0:T(8,128)} %bitcast.37, bf16[2304,1152]{1,0:T(8,128)(2,1)} %bitcast.38, bf16[2304,1152]{1,0:T(8,128)(2,1)} %bitcast.41, f32[1,1152]{1,0:T(1,128)} %broadcast_in_dim.20.gain_ref, f32[1024,1]{1,0:T(8,128)} %copy.15.keep_ref), custom_call_target="tpu_custom_call" | custom-call | flops 16307453952 | bytes 20054016 | tf_op jit(solution)/shard_map/source/pallas_call | solution.py:154
  218.2 1.8 fusion.10
  220.0 1.9 collective-permute-start.5
  221.9 0.0 collective-permute-start.4
  221.9 7.4 %collective-permute-done.5.right_ref = f32[32,4,1152]{2,1,0:T(4,128)S(1)} collective-permute-done((f32[32,4,1152]{2,1,0:T(4,128)S(1)}, f32[32,4,1152]{2,1,0:T(4,128)S(1)}, u32[]{:S(2)}, u32[]{:S(2)}) %collective-permute-start.5) | collective-permute-done | bytes 589856 | tf_op jit(solution)/shard_map/ppermute | solution.py:360
  229.3 2.5 collective-permute-done.4.left_ref
  231.8 2.3 copy-done.2
  234.2 22.9 %advect.3 = f32[32,32,1152]{2,1,0:T(8,128)S(1)} custom-call(f32[1,1152]{1,0:T(1,128)S(1)} %get-tuple-element.24.cx_ref, f32[1,1152]{1,0:T(1,128)S(1)} %get-tuple-element.23.cy_ref, f32[32,40,128]{2,1,0:T(8,128)S(1)} %broadcast_in_dim.16.uf_ref, f32[33,40,128]{2,1,0:T(8,128)S(1)} %broadcast_in_dim.17.vf_ref, f32[33,40,128]{2,1,0:T(8,128)S(1)} %broadcast_in_dim.18.flag_ref, ...), custom_call_target="tpu_custom_call" | custom-call | tf_op jit(solution)/shard_map/advect/pallas_call | solution.py:92
  257.0 0.0 copy-start.3
  257.1 2.2 copy-done.3
  259.2 16.5 %source.5 = f32[2,1152,256]{2,1,0:T(8,128)} custom-call(f32[1024,1152]{1,0:T(8,128)} %bitcast.35, bf16[2304,1152]{1,0:T(8,128)(2,1)} %bitcast.39, bf16[2304,1152]{1,0:T(8,128)(2,1)} %bitcast.42, f32[1,1152]{1,0:T(1,128)} %broadcast_in_dim.20.gain_ref, f32[1024,1]{1,0:T(8,128)} %copy.15.keep_ref), custom_call_target="tpu_custom_call" | custom-call | flops 8153726976 | bytes 15335424 | tf_op jit(solution)/shard_map/source/pallas_call | solution.py:154
  275.7 9.7 %all-to-all-start.2 = ((f32[32,72,256]{2,1,0:T(8,128)}), f32[32,72,256]{2,1,0:T(8,128)S(1)}, u32[]{:S(2)}, u32[]{:S(2)}) async-start(f32[32,72,256]{2,1,0:T(8,128)} %bitcast.44), calls=%async_computation.2 | async-start | bytes 4718592 | tf_op jit(solution)/shard_map/all_to_all | solution.py:370
  285.4 16.6 %source.4 = f32[2,1152,256]{2,1,0:T(8,128)} custom-call(f32[1024,1152]{1,0:T(8,128)} %bitcast.36, bf16[2304,1152]{1,0:T(8,128)(2,1)} %bitcast.40, bf16[2304,1152]{1,0:T(8,128)(2,1)} %bitcast.43, f32[1,1152]{1,0:T(1,128)} %broadcast_in_dim.20.gain_ref, f32[1024,1]{1,0:T(8,128)} %copy.15.keep_ref), custom_call_target="tpu_custom_call" | custom-call | flops 8153726976 | bytes 15335424 | tf_op jit(solution)/shard_map/source/pallas_call | solution.py:154
  302.0 38.8 %all-to-all-done.2.lower_ref = f32[32,72,256]{2,1,0:T(8,128)S(1)} async-done(((f32[32,72,256]{2,1,0:T(8,128)}), f32[32,72,256]{2,1,0:T(8,128)S(1)}, u32[]{:S(2)}, u32[]{:S(2)}) %all-to-all-start.2) | async-done | bytes 2359328 | tf_op jit(solution)/shard_map/all_to_all | solution.py:370
  340.8 58.9 %all_to_all.15.upper_ref = f32[32,72,256]{2,1,0:T(8,128)} all-to-all(f32[32,72,256]{2,1,0:T(8,128)} %bitcast.45), channel_id=1, replica_groups=mesh['lat'=2,'comp'=16] {'lat','comp'}, dimensions={0} | all-to-all | bytes 4718592 | tf_op jit(solution)/shard_map/all_to_all | solution.py:370
  399.6 9.3 %join.1 = f32[72,16,1024]{2,1,0:T(8,128)} custom-call(f32[32,72,256]{2,1,0:T(8,128)} %all_to_all.15.upper_ref, f32[32,72,256]{2,1,0:T(8,128)} %copy-done.7), custom_call_target="tpu_custom_call" | custom-call | tf_op jit(solution)/shard_map/join/pallas_call | solution.py:246
  (19 shorter events, 0.1 us)
Async XLA Ops:
  11.3 117.8 %copy-start.9 = (s32[16,1024]{1,0:T(8,128)S(1)}, s32[16,1024]{1,0:T(8,128)}, u32[]{:S(2)}) copy-start(s32[16,1024]{1,0:T(8,128)} %param.13) | copy-start | bytes 196612
  11.3 117.8 %copy-start.10 = (s32[16,1024]{1,0:T(8,128)S(1)}, s32[16,1024]{1,0:T(8,128)}, u32[]{:S(2)}) copy-start(s32[16,1024]{1,0:T(8,128)} %param.14) | copy-start | bytes 196612
  11.3 117.8 %copy-start.8 = (f32[2,16,1024]{2,1,0:T(8,128)S(1)}, f32[2,16,1024]{2,1,0:T(8,128)}, u32[]{:S(2)}) copy-start(f32[2,16,1024]{2,1,0:T(8,128)} %param.12) | copy-start | bytes 393220
  11.3 127.9 %copy-start.12 = (s32[1024]{0:T(1024)S(1)}, s32[1024]{0:T(1024)}, u32[]{:S(2)}) copy-start(s32[1024]{0:T(1024)} %param.15) | copy-start | bytes 12292
  11.3 128.6 %all-to-all-start = ((f32[32,72,512]{2,1,0:T(8,128)}), f32[32,72,512]{2,1,0:T(8,128)}, u32[]{:S(2)}, u32[]{:S(2)}) async-start(f32[32,72,512]{2,1,0:T(8,128)} %split.1), calls=%async_computation | async-start | bytes 9437184 | tf_op jit(solution)/shard_map/all_to_all | solution.py:324
  18.8 110.3 %collective-permute-start.2 = (f32[576,1152]{1,0:T(8,128)S(1)}, f32[576,1152]{1,0:T(8,128)}, u32[]{:S(2)}, u32[]{:S(2)}) collective-permute-start(f32[576,1152]{1,0:T(8,128)S(1)} %broadcast_select_fusion), channel_id=1, source_target_pairs={{0,16},{16,0},{1,17},{17,1},{2,18},{18,2},{3,19},{19,3},{4,20},{20... | collective-permute-start | bytes 7962632 | tf_op jit(solution)/shard_map/ppermute | solution.py:322
  129.1 22.4 %collective-permute-start.3 = (f32[576,1152]{1,0:T(8,128)}, f32[576,1152]{1,0:T(8,128)}, u32[]{:S(2)}, u32[]{:S(2)}) collective-permute-start(f32[576,1152]{1,0:T(8,128)} %collective-permute-done.2.fetched_ref), channel_id=1, source_target_pairs={{0,1},{1,0},{2,3},{3,2},{4,5},{5,4},{6,7},{7,6},{8,9},{9,8},{10,11... | collective-permute-start | bytes 7962632 | tf_op jit(solution)/shard_map/ppermute | solution.py:281
  139.9 9.7 %copy-start.11 = (f32[1152]{0:T(1024)S(1)}, f32[1152]{0:T(1024)}, u32[]{:S(2)}) copy-start(f32[1152]{0:T(1024)} %param.11) | copy-start | bytes 13828
  139.9 11.6 %copy-start = (f32[576,1152]{1,0:T(8,128)S(1)}, f32[576,1152]{1,0:T(8,128)}, u32[]{:S(2)}) copy-start(f32[576,1152]{1,0:T(8,128)} %plus_ref.1) | copy-start | bytes 7962628
  149.0 15.2 %collective-permute-start.1 = (f32[32,4,1152]{2,1,0:T(4,128)}, f32[32,4,1152]{2,1,0:T(4,128)S(1)}, u32[]{:S(2)}, u32[]{:S(2)}) collective-permute-start(f32[32,4,1152]{2,1,0:T(4,128)} %get-tuple-element.15), channel_id=1, source_target_pairs={{1,0},{2,1},{3,2},{4,3},{5,4},{6,5},{7,6},{8,7},{9,8},{10,9},{11,1... | collective-permute-start | bytes 1769480 | tf_op jit(solution)/shard_map/ppermute | solution.py:360
  149.4 14.8 %collective-permute-start = (f32[32,4,1152]{2,1,0:T(4,128)}, f32[32,4,1152]{2,1,0:T(4,128)}, u32[]{:S(2)}, u32[]{:S(2)}) collective-permute-start(f32[32,4,1152]{2,1,0:T(4,128)} %get-tuple-element.16), channel_id=1, source_target_pairs={{0,1},{1,2},{2,3},{3,4},{4,5},{5,6},{6,7},{7,8},{8,9},{9,10},{10,1... | collective-permute-start | bytes 1769480 | tf_op jit(solution)/shard_map/ppermute | solution.py:359
  151.4 13.7 %slice-start = ((s8[4718592]{0:T(1024)(128)(4,1)}), s8[4194304]{0:T(1024)(128)(4,1)S(1)}, s32[]{:S(2)}) async-start(s8[4718592]{0:T(1024)(128)(4,1)} %bitcast.30), calls=%async_computation.3 | async-start | bytes 8388608
  151.5 13.7 %slice-start.1 = ((s8[4718592]{0:T(1024)(128)(4,1)}), s8[524288]{0:T(1024)(128)(4,1)S(1)}, s32[]{:S(2)}) async-start(s8[4718592]{0:T(1024)(128)(4,1)} %bitcast.30), calls=%async_computation.4 | async-start | bytes 1048576
  151.5 1.9 copy-start.1
  159.4 2.4 copy-start.5
  161.8 2.4 copy-start.6
  188.8 2.2 copy-start.4
  220.0 9.3 %collective-permute-start.5 = (f32[32,4,1152]{2,1,0:T(4,128)S(1)}, f32[32,4,1152]{2,1,0:T(4,128)S(1)}, u32[]{:S(2)}, u32[]{:S(2)}) collective-permute-start(f32[32,4,1152]{2,1,0:T(4,128)S(1)} %get-tuple-element.13), channel_id=1, source_target_pairs={{1,0},{2,1},{3,2},{4,3},{5,4},{6,5},{7,6},{8,7},{9,8},{10,9},{11,1... | collective-permute-start | bytes 1769480 | tf_op jit(solution)/shard_map/ppermute | solution.py:360
  221.9 9.9 %collective-permute-start.4 = (f32[32,4,1152]{2,1,0:T(4,128)S(1)}, f32[32,4,1152]{2,1,0:T(4,128)S(1)}, u32[]{:S(2)}, u32[]{:S(2)}) collective-permute-start(f32[32,4,1152]{2,1,0:T(4,128)S(1)} %get-tuple-element.14), channel_id=1, source_target_pairs={{0,1},{1,2},{2,3},{3,4},{4,5},{5,6},{6,7},{7,8},{8,9},{9,10},{10,1... | collective-permute-start | bytes 1769480 | tf_op jit(solution)/shard_map/ppermute | solution.py:359
  231.8 2.3 copy-start.2
  257.0 2.2 copy-start.3
  275.7 65.0 %all-to-all-start.2 = ((f32[32,72,256]{2,1,0:T(8,128)}), f32[32,72,256]{2,1,0:T(8,128)S(1)}, u32[]{:S(2)}, u32[]{:S(2)}) async-start(f32[32,72,256]{2,1,0:T(8,128)} %bitcast.44), calls=%async_computation.2 | async-start | bytes 4718592 | tf_op jit(solution)/shard_map/all_to_all | solution.py:370
  340.8 58.9 %copy-start.7 = (f32[32,72,256]{2,1,0:T(8,128)}, f32[32,72,256]{2,1,0:T(8,128)S(1)}, u32[]{:S(2)}) copy-start(f32[32,72,256]{2,1,0:T(8,128)S(1)} %all-to-all-done.2.lower_ref) | copy-start | bytes 7077892

commit v4 on v3

--- a/solution.py
+++ b/solution.py
@@ -145,7 +145,7 @@
         result = jax.ShapeDtypeStruct((bands, comps, tile), jnp.float32)
         out_spec = pl.BlockSpec((1, comps, tile), lambda p: (p, 0, 0))
     else:
-        tile = min(256, points)
+        tile = min(512, points)
         grid = (points // tile,)
         place = lambda p: (p, 0)
         result = jax.ShapeDtypeStruct(field.shape, jnp.float32)
@@ -328,7 +328,11 @@
     statics = jnp.stack(
         [current[0], current[1], limiter_flags.astype(jnp.float32), sea_mask.astype(jnp.float32)]
     )
-    statics = lax.all_gather(statics, "lat", axis=1, tiled=True)
+    beside = lax.ppermute(statics, "lat", [(0, 1), (1, 0)])
+    first = lat_rank == 0
+    statics = jnp.concatenate(
+        [jnp.where(first, statics, beside), jnp.where(first, beside, statics)], axis=1
+    )
     wide = lons + 2 * HALO
     ring = jnp.concatenate([statics[:, :, -HALO:], statics, statics[:, :, : HALO + 1]], axis=2)
     window = lax.dynamic_slice(ring, (0, 0, block * lons), (4, rows, wide + 1))

time: 410 us -> 411 us (level)
  blocking collectives: 68.3 us -> 58.9 us
  other arithmetic: 3.13 us -> 8.07 us
    all_gather x1 -> x0, blocking collectives: 9.39 us -> none  [body(): statics = lax.all_gather(statics, 'lat', axis=1, tiled=True)]
    unnamed x30 -> x32, local copies, waits for them, and re-layouts: 13.4 us -> 13.4 us
  transfers between devices with their start and end apart: 8 -> 9, of which waited for: 4 -> 5; matrix products, arithmetic and copies ran while one was open for 3% -> 5% of each run, Pallas kernels for 6% -> 6%
where the time goes in v4:
time: 411 us; the launch traced here: 410 us
  waiting for transfers between devices  160 us (39%)
  Pallas kernels  131 us (32%)
  blocking collectives  58.9 us (14%)
  local copies, waits for them, and re-layouts  29.9 us (7%)
  starting transfers between devices  21.7 us (5%)
  other arithmetic  8.07 us (2%)
    ppermute x1, waiting for transfers between devices, body(): fetched = lax.ppermute(send, 'lat', [(0, 1), (1, 0)])  109 us
    pallas_call x3, Pallas kernels, source(): pl.pallas_call(functools.partial(source_kernel, bands > 0), grid=grid, ou...  60.2 us
    all_to_all x1, blocking collectives, body(): lax.all_to_all(spread, BOTH, split_axis=0, concat_axis=0, tiled=True)  58.9 us
    pallas_call x2, Pallas kernels, advect(): pl.pallas_call(advect_kernel, grid=(comps // LANES,), out_shape=jax.Shape...  46.5 us
    all_to_all x2, waiting for transfers between devices, body(): lax.all_to_all(spread, BOTH, split_axis=0, concat_axis=0, tiled=True)  38.8 us
    all_to_all x2, starting transfers between devices, body(): lax.all_to_all(spread, BOTH, split_axis=0, concat_axis=0, tiled=True)  17.1 us
    unnamed x32, local copies, waits for them, and re-layouts  13.4 us
    pallas_call x1, Pallas kernels, join(): pl.pallas_call(functools.partial(join_kernel, order, width), grid=(local_...  9.33 us
  transfers between devices with their start and end apart: 9, of which 5 were waited for; matrix products, arithmetic and copies ran while one was open for 5% of the time, Pallas kernels for 6%

profile of v4, /device:TPU:0, one launch (start us, length us, event | category | flops | bytes accessed | tf_op | source)
XLA Modules:
  0.0 409.7 jit_solution(1745096202714671323)
XLA Ops:
  0.0 2.0 broadcast_select_fusion
  2.0 9.3 %split.1 = f32[32,72,512]{2,1,0:T(8,128)} custom-call(f32[72,16,1024]{2,1,0:T(8,128)} %field_ref), custom_call_target="tpu_custom_call" | custom-call | tf_op jit(solution)/shard_map/split/pallas_call | solution.py:229
  11.3 0.0 copy-start.12
  11.4 7.4 %all-to-all-start = ((f32[32,72,512]{2,1,0:T(8,128)}), f32[32,72,512]{2,1,0:T(8,128)}, u32[]{:S(2)}, u32[]{:S(2)}) async-start(f32[32,72,512]{2,1,0:T(8,128)} %split.1), calls=%async_computation | async-start | bytes 9437184 | tf_op jit(solution)/shard_map/all_to_all | solution.py:324
  18.8 1.8 collective-permute-start.3
  20.6 0.4 collective-permute-start
  21.0 108.6 %collective-permute-done.3.fetched_ref = f32[576,1152]{1,0:T(8,128)} collective-permute-done((f32[576,1152]{1,0:T(8,128)S(1)}, f32[576,1152]{1,0:T(8,128)}, u32[]{:S(2)}, u32[]{:S(2)}) %collective-permute-start.3) | collective-permute-done | bytes 2654240 | tf_op jit(solution)/shard_map/ppermute | solution.py:322
  129.5 0.0 collective-permute-start.4
  129.6 0.1 iota_add_fusion
  129.6 0.1 add.144
  129.7 0.0 copy-done.13
  129.7 0.7 compare_reduce_fusion
  130.4 0.1 pad_add_fusion.rank_ref
  130.5 0.6 broadcast_in_dim.20.gain_ref
  131.1 1.0 copy.15.keep_ref
  132.1 0.2 sine_multiply_fusion
  132.3 2.4 collective-permute-done
  134.7 1.0 broadcast_select_fusion.1
  135.7 0.7 fusion
  136.4 0.0 all-to-all-done
  136.4 6.0 %copy.14 = f32[2,1152,512]{1,2,0:T(8,128)} copy(f32[2,1152,512]{2,1,0:T(8,128)} %bitcast.6) | data formatting | bytes 9437184 | tf_op jit(solution)/shard_map/reshape | solution.py:325
  142.5 0.0 copy-done.8
  142.5 3.0 fusion.13
  145.5 0.4 collective-permute-start.2
  145.8 0.2 collective-permute-start.1
  146.0 1.4 fusion.1
  147.4 1.8 pad_maximum_fusion
  149.2 2.1 concatenate.7
  151.3 0.9 dynamic-slice_bitcast_fusion
  152.2 0.0 slice-start
  152.3 0.1 fusion.4
  152.3 0.0 collective-permute-done.4.shared_ref
  152.3 0.0 copy-start.1
  152.4 1.9 copy-done.1
  154.2 6.0 %maps.1 = (bf16[4,576,1152]{2,1,0:T(8,128)(2,1)S(1)}, bf16[4,576,1152]{2,1,0:T(8,128)(2,1)S(1)}) custom-call(s32[2]{0:T(128)S(1)} %pad_add_fusion.rank_ref, f32[576,1152]{1,0:T(8,128)S(1)} %copy-done, f32[576,1152]{1,0:T(8,128)S(1)} %copy-done.1, f32[576,1152]{1,0:T(8,128)} %collective-permute-done.3.fetched_ref, f32[576,1152]{1,0:T(8,128)} %collective-permute-done.4.shared_ref), custom_call_target="tpu_custom_call" | custom-call | tf_op jit(solution)/shard_map/maps/pallas_call | solution.py:285
  160.2 0.0 copy-start.5
  160.3 2.3 copy-done.5
  162.6 2.4 copy-done.6
  165.0 0.0 collective-permute-done.2.right_ref
  165.0 0.0 collective-permute-done.1.left_ref
  165.0 0.2 broadcast_in_dim.16.uf_ref
  165.2 0.2 broadcast_in_dim.19.sea_ref
  165.5 0.2 broadcast_in_dim.17.vf_ref
  165.7 0.2 broadcast_in_dim.18.flag_ref
  166.0 0.0 slice-done
  166.0 23.6 %advect.2 = f32[32,32,1152]{2,1,0:T(8,128)S(1)} custom-call(f32[1,1152]{1,0:T(1,128)S(1)} %get-tuple-element.26.cx_ref, f32[1,1152]{1,0:T(1,128)S(1)} %get-tuple-element.25.cy_ref, f32[32,40,128]{2,1,0:T(8,128)S(1)} %broadcast_in_dim.16.uf_ref, f32[33,40,128]{2,1,0:T(8,128)S(1)} %broadcast_in_dim.17.vf_ref, f32[33,40,128]{2,1,0:T(8,128)S(1)} %broadcast_in_dim.18.flag_ref, ...), custom_call_target="tpu_custom_call" | custom-call | tf_op jit(solution)/shard_map/advect/pallas_call | solution.py:92
  189.6 0.0 copy-start.4
  189.6 2.2 copy-done.4
  191.8 27.2 %source.3 = f32[1024,1152]{1,0:T(8,128)} custom-call(f32[1024,1152]{1,0:T(8,128)} %bitcast.37, bf16[2304,1152]{1,0:T(8,128)(2,1)} %bitcast.38, bf16[2304,1152]{1,0:T(8,128)(2,1)} %bitcast.41, f32[1,1152]{1,0:T(1,128)} %broadcast_in_dim.20.gain_ref, f32[1024,1]{1,0:T(8,128)} %copy.15.keep_ref), custom_call_target="tpu_custom_call" | custom-call | flops 16307453952 | bytes 20054016 | tf_op jit(solution)/shard_map/source/pallas_call | solution.py:154
  219.0 1.8 fusion.12
  220.8 1.9 collective-permute-start.6
  222.7 0.0 collective-permute-start.5
  222.7 7.4 %collective-permute-done.6.right_ref = f32[32,4,1152]{2,1,0:T(4,128)S(1)} collective-permute-done((f32[32,4,1152]{2,1,0:T(4,128)S(1)}, f32[32,4,1152]{2,1,0:T(4,128)S(1)}, u32[]{:S(2)}, u32[]{:S(2)}) %collective-permute-start.6) | collective-permute-done | bytes 589856 | tf_op jit(solution)/shard_map/ppermute | solution.py:364
  230.1 2.5 collective-permute-done.5.left_ref
  232.6 2.3 copy-done.2
  235.0 22.9 %advect.3 = f32[32,32,1152]{2,1,0:T(8,128)S(1)} custom-call(f32[1,1152]{1,0:T(1,128)S(1)} %get-tuple-element.26.cx_ref, f32[1,1152]{1,0:T(1,128)S(1)} %get-tuple-element.25.cy_ref, f32[32,40,128]{2,1,0:T(8,128)S(1)} %broadcast_in_dim.16.uf_ref, f32[33,40,128]{2,1,0:T(8,128)S(1)} %broadcast_in_dim.17.vf_ref, f32[33,40,128]{2,1,0:T(8,128)S(1)} %broadcast_in_dim.18.flag_ref, ...), custom_call_target="tpu_custom_call" | custom-call | tf_op jit(solution)/shard_map/advect/pallas_call | solution.py:92
  257.8 0.0 copy-start.3
  257.9 2.2 copy-done.3
  260.0 16.5 %source.5 = f32[2,1152,256]{2,1,0:T(8,128)} custom-call(f32[1024,1152]{1,0:T(8,128)} %bitcast.35, bf16[2304,1152]{1,0:T(8,128)(2,1)} %bitcast.39, bf16[2304,1152]{1,0:T(8,128)(2,1)} %bitcast.42, f32[1,1152]{1,0:T(1,128)} %broadcast_in_dim.20.gain_ref, f32[1024,1]{1,0:T(8,128)} %copy.15.keep_ref), custom_call_target="tpu_custom_call" | custom-call | flops 8153726976 | bytes 15335424 | tf_op jit(solution)/shard_map/source/pallas_call | solution.py:154
  276.5 9.7 %all-to-all-start.2 = ((f32[32,72,256]{2,1,0:T(8,128)}), f32[32,72,256]{2,1,0:T(8,128)S(1)}, u32[]{:S(2)}, u32[]{:S(2)}) async-start(f32[32,72,256]{2,1,0:T(8,128)} %bitcast.44), calls=%async_computation.2 | async-start | bytes 4718592 | tf_op jit(solution)/shard_map/all_to_all | solution.py:374
  286.2 16.6 %source.4 = f32[2,1152,256]{2,1,0:T(8,128)} custom-call(f32[1024,1152]{1,0:T(8,128)} %bitcast.36, bf16[2304,1152]{1,0:T(8,128)(2,1)} %bitcast.40, bf16[2304,1152]{1,0:T(8,128)(2,1)} %bitcast.43, f32[1,1152]{1,0:T(1,128)} %broadcast_in_dim.20.gain_ref, f32[1024,1]{1,0:T(8,128)} %copy.15.keep_ref), custom_call_target="tpu_custom_call" | custom-call | flops 8153726976 | bytes 15335424 | tf_op jit(solution)/shard_map/source/pallas_call | solution.py:154
  302.8 38.8 %all-to-all-done.2.lower_ref = f32[32,72,256]{2,1,0:T(8,128)S(1)} async-done(((f32[32,72,256]{2,1,0:T(8,128)}), f32[32,72,256]{2,1,0:T(8,128)S(1)}, u32[]{:S(2)}, u32[]{:S(2)}) %all-to-all-start.2) | async-done | bytes 2359328 | tf_op jit(solution)/shard_map/all_to_all | solution.py:374
  341.5 58.9 %all_to_all.15.upper_ref = f32[32,72,256]{2,1,0:T(8,128)} all-to-all(f32[32,72,256]{2,1,0:T(8,128)} %bitcast.45), channel_id=1, replica_groups=mesh['lat'=2,'comp'=16] {'lat','comp'}, dimensions={0} | all-to-all | bytes 4718592 | tf_op jit(solution)/shard_map/all_to_all | solution.py:374
  400.4 9.3 %join.1 = f32[72,16,1024]{2,1,0:T(8,128)} custom-call(f32[32,72,256]{2,1,0:T(8,128)} %all_to_all.15.upper_ref, f32[32,72,256]{2,1,0:T(8,128)} %copy-done.7), custom_call_target="tpu_custom_call" | custom-call | tf_op jit(solution)/shard_map/join/pallas_call | solution.py:246
  (24 shorter events, 0.1 us)
Async XLA Ops:
  11.3 9.2 %copy-start.10 = (s32[16,1024]{1,0:T(8,128)S(1)}, s32[16,1024]{1,0:T(8,128)}, u32[]{:S(2)}) copy-start(s32[16,1024]{1,0:T(8,128)} %param.13) | copy-start | bytes 196612
  11.3 9.2 %copy-start.11 = (s32[16,1024]{1,0:T(8,128)S(1)}, s32[16,1024]{1,0:T(8,128)}, u32[]{:S(2)}) copy-start(s32[16,1024]{1,0:T(8,128)} %param.14) | copy-start | bytes 196612
  11.3 9.2 %copy-start.9 = (f32[2,16,1024]{2,1,0:T(8,128)S(1)}, f32[2,16,1024]{2,1,0:T(8,128)}, u32[]{:S(2)}) copy-start(f32[2,16,1024]{2,1,0:T(8,128)} %param.12) | copy-start | bytes 393220
  11.3 118.4 %copy-start.13 = (s32[1024]{0:T(1024)S(1)}, s32[1024]{0:T(1024)}, u32[]{:S(2)}) copy-start(s32[1024]{0:T(1024)} %param.15) | copy-start | bytes 12292
  11.3 119.1 %copy-start.12 = (f32[1152]{0:T(1024)S(1)}, f32[1152]{0:T(1024)}, u32[]{:S(2)}) copy-start(f32[1152]{0:T(1024)} %param.11) | copy-start | bytes 13828
  11.4 125.1 %all-to-all-start = ((f32[32,72,512]{2,1,0:T(8,128)}), f32[32,72,512]{2,1,0:T(8,128)}, u32[]{:S(2)}, u32[]{:S(2)}) async-start(f32[32,72,512]{2,1,0:T(8,128)} %split.1), calls=%async_computation | async-start | bytes 9437184 | tf_op jit(solution)/shard_map/all_to_all | solution.py:324
  18.8 110.8 %collective-permute-start.3 = (f32[576,1152]{1,0:T(8,128)S(1)}, f32[576,1152]{1,0:T(8,128)}, u32[]{:S(2)}, u32[]{:S(2)}) collective-permute-start(f32[576,1152]{1,0:T(8,128)S(1)} %broadcast_select_fusion), channel_id=1, source_target_pairs={{0,16},{16,0},{1,17},{17,1},{2,18},{18,2},{3,19},{19,3},{4,20},{20... | collective-permute-start | bytes 7962632 | tf_op jit(solution)/shard_map/ppermute | solution.py:322
  20.6 114.1 %collective-permute-start = (f32[4,16,1024]{2,1,0:T(8,128)S(1)}, f32[4,16,1024]{2,1,0:T(8,128)}, u32[]{:S(2)}, u32[]{:S(2)}) collective-permute-start(f32[4,16,1024]{2,1,0:T(8,128)S(1)} %pad_maximum_fusion.1), channel_id=1, source_target_pairs={{0,16},{16,0},{1,17},{17,1},{2,18},{18,2},{3,19},{19,3},{4,20},{20... | collective-permute-start | bytes 786440 | tf_op jit(solution)/shard_map/ppermute | solution.py:331
  129.5 22.8 %collective-permute-start.4 = (f32[576,1152]{1,0:T(8,128)}, f32[576,1152]{1,0:T(8,128)}, u32[]{:S(2)}, u32[]{:S(2)}) collective-permute-start(f32[576,1152]{1,0:T(8,128)} %collective-permute-done.3.fetched_ref), channel_id=1, source_target_pairs={{0,1},{1,0},{2,3},{3,2},{4,5},{5,4},{6,7},{7,6},{8,9},{9,8},{10,11... | collective-permute-start | bytes 7962632 | tf_op jit(solution)/shard_map/ppermute | solution.py:281
  135.7 6.8 %copy-start.8 = (f32[4,16,1024]{2,1,0:T(8,128)}, f32[4,16,1024]{2,1,0:T(8,128)S(1)}, u32[]{:S(2)}) copy-start(f32[4,16,1024]{2,1,0:T(8,128)S(1)} %get-tuple-element.22) | copy-start | bytes 786436
  142.5 9.8 %copy-start = (f32[576,1152]{1,0:T(8,128)S(1)}, f32[576,1152]{1,0:T(8,128)}, u32[]{:S(2)}) copy-start(f32[576,1152]{1,0:T(8,128)} %plus_ref.1) | copy-start | bytes 7962628
  145.5 19.5 %collective-permute-start.2 = (f32[32,4,1152]{2,1,0:T(4,128)}, f32[32,4,1152]{2,1,0:T(4,128)S(1)}, u32[]{:S(2)}, u32[]{:S(2)}) collective-permute-start(f32[32,4,1152]{2,1,0:T(4,128)} %get-tuple-element.15), channel_id=1, source_target_pairs={{1,0},{2,1},{3,2},{4,3},{5,4},{6,5},{7,6},{8,7},{9,8},{10,9},{11,1... | collective-permute-start | bytes 1769480 | tf_op jit(solution)/shard_map/ppermute | solution.py:364
  145.8 19.2 %collective-permute-start.1 = (f32[32,4,1152]{2,1,0:T(4,128)}, f32[32,4,1152]{2,1,0:T(4,128)}, u32[]{:S(2)}, u32[]{:S(2)}) collective-permute-start(f32[32,4,1152]{2,1,0:T(4,128)} %get-tuple-element.16), channel_id=1, source_target_pairs={{0,1},{1,2},{2,3},{3,4},{4,5},{5,6},{6,7},{7,8},{8,9},{9,10},{10,1... | collective-permute-start | bytes 1769480 | tf_op jit(solution)/shard_map/ppermute | solution.py:363
  152.2 13.7 %slice-start = ((s8[4718592]{0:T(1024)(128)(4,1)}), s8[4194304]{0:T(1024)(128)(4,1)S(1)}, s32[]{:S(2)}) async-start(s8[4718592]{0:T(1024)(128)(4,1)} %bitcast.30), calls=%async_computation.3 | async-start | bytes 8388608
  152.3 13.7 %slice-start.1 = ((s8[4718592]{0:T(1024)(128)(4,1)}), s8[524288]{0:T(1024)(128)(4,1)S(1)}, s32[]{:S(2)}) async-start(s8[4718592]{0:T(1024)(128)(4,1)} %bitcast.30), calls=%async_computation.4 | async-start | bytes 1048576
  152.3 1.9 copy-start.1
  160.2 2.3 copy-start.5
  162.6 2.4 copy-start.6
  189.6 2.2 copy-start.4
  220.8 9.3 %collective-permute-start.6 = (f32[32,4,1152]{2,1,0:T(4,128)S(1)}, f32[32,4,1152]{2,1,0:T(4,128)S(1)}, u32[]{:S(2)}, u32[]{:S(2)}) collective-permute-start(f32[32,4,1152]{2,1,0:T(4,128)S(1)} %get-tuple-element.13), channel_id=1, source_target_pairs={{1,0},{2,1},{3,2},{4,3},{5,4},{6,5},{7,6},{8,7},{9,8},{10,9},{11,1... | collective-permute-start | bytes 1769480 | tf_op jit(solution)/shard_map/ppermute | solution.py:364
  222.7 9.9 %collective-permute-start.5 = (f32[32,4,1152]{2,1,0:T(4,128)S(1)}, f32[32,4,1152]{2,1,0:T(4,128)S(1)}, u32[]{:S(2)}, u32[]{:S(2)}) collective-permute-start(f32[32,4,1152]{2,1,0:T(4,128)S(1)} %get-tuple-element.14), channel_id=1, source_target_pairs={{0,1},{1,2},{2,3},{3,4},{4,5},{5,6},{6,7},{7,8},{8,9},{9,10},{10,1... | collective-permute-start | bytes 1769480 | tf_op jit(solution)/shard_map/ppermute | solution.py:363
  232.6 2.3 copy-start.2
  257.8 2.2 copy-start.3
  276.5 65.0 %all-to-all-start.2 = ((f32[32,72,256]{2,1,0:T(8,128)}), f32[32,72,256]{2,1,0:T(8,128)S(1)}, u32[]{:S(2)}, u32[]{:S(2)}) async-start(f32[32,72,256]{2,1,0:T(8,128)} %bitcast.44), calls=%async_computation.2 | async-start | bytes 4718592 | tf_op jit(solution)/shard_map/all_to_all | solution.py:374
  341.5 58.9 %copy-start.7 = (f32[32,72,256]{2,1,0:T(8,128)}, f32[32,72,256]{2,1,0:T(8,128)S(1)}, u32[]{:S(2)}) copy-start(f32[32,72,256]{2,1,0:T(8,128)S(1)} %all-to-all-done.2.lower_ref) | copy-start | bytes 7077892
